TPU v7x, 128 devices: a whole 4x4x4 slice. The times are simulated.
128 devices in a mesh: airway: 8 (over y, core), section: 16 (over z, x).
Axes of the slice: x: 4, y: 4, z: 4, core: 2. Of those that a mesh axis runs over, the one named last changes fastest.
Arguments:
- fluid_velocity: float32 [3, 64, 128, 2048], P(None, None, 'section', 'airway'), may hold values from -6 to 6
- viscosity: float32 [128, 2048], P('section', 'airway'), may hold values from 0.002 to 0.008
- axial_speed: float32 [128, 2048], P('section', 'airway'), may hold values from 0.01 to 0.04
- fluid_mass: float32 [128, 2048], P('section', 'airway'), may hold values from 2 to 8
- positions: float32 [24576, 3, 128], P(('airway', 'section')), may hold values from -1 to 1
- velocities: float32 [24576, 3, 128], P(('airway', 'section')), may hold values from -6 to 6
- relax_rates: float32 [24576, 128], P(('airway', 'section')), may hold values from 0.02 to 0.5
- bin_element: int32 [24576], P(('airway', 'section')), may hold values from 0 to 2047
- bin_fill: int32 [24576], P(('airway', 'section')), may hold values from 0 to 128, as said below
Outputs:
- fluid_out: float32 [3, 64, 128, 2048], P(None, None, 'section', 'airway')
- particles_out: float32 [24576, 6, 128], P(('airway', 'section'))
Inputs may be any that keep to these rules, and one draw needn't show every extreme that they name: `bin_fill`: on each device the bins with particles are the first 64 + k slots, k from 0 to 128; over all devices the k sum to exactly 8192, and k = 128 on some device. Every device's first slot holds 128 particles.
All inputs are finite; a program needn't handle non-finite values.
Results may differ from a plain program's by a relative error of at most 0.00023.
Values sent between devices are 32-bit elements; how exact they have to be, the bound alone decides.
A program may use at most 64 MiB of HBM per device.

v0:
```python
import jax
import jax.numpy as jnp
import numpy as np
from jax import lax
from jax.sharding import PartitionSpec as P

NODES = 64
SUBSTEPS = 16
PASSES = 4
HOME = 64


node_coords = (-1.0, -1.0 / 3.0, 1.0 / 3.0, 1.0)
penalty_weight = 0.25
stride_step = 0.05
exact_mode = lax.Precision.HIGHEST


def with_halo(cells, sides, width):
    for axis, dim in sides:
        count = lax.axis_size(axis)
        ends = count - 1
        head = lax.slice_in_dim(cells, 0, width, axis=dim)
        tail = lax.slice_in_dim(cells, cells.shape[dim] - width, cells.shape[dim], axis=dim)
        cells = jnp.concatenate(
            [
                lax.ppermute(tail, axis, [(i, (i + 1) % count) for i in range(ends)]),
                cells,
                lax.ppermute(head, axis, [((i + 1) % count, i) for i in range(ends)]),
            ],
            axis=dim,
        )
    return cells


def deriv_table():
    matrix = np.zeros((4, 4))
    for row_node in range(4):
        for col_node in range(4):
            summed = 0.0
            for skip_node in range(4):
                if skip_node != col_node:
                    factor = 1.0 / (node_coords[col_node] - node_coords[skip_node])
                    for third_node in range(4):
                        if third_node != col_node and third_node != skip_node:
                            factor = (
                                factor
                                * (node_coords[row_node] - node_coords[third_node])
                                / (node_coords[col_node] - node_coords[third_node])
                            )
                    summed = summed + factor
            matrix[row_node, col_node] = summed
    return matrix


def operator_table():
    first_deriv = deriv_table()
    second_deriv = first_deriv @ first_deriv
    identity = np.eye(4)
    laplace = (
        np.kron(np.kron(second_deriv, identity), identity)
        + np.kron(np.kron(identity, second_deriv), identity)
        + np.kron(np.kron(identity, identity), second_deriv)
    )
    airway_grad = np.kron(np.kron(first_deriv, identity), identity)
    return np.concatenate([laplace, airway_grad], axis=0).astype(np.float32)


def basis_values(coordinate):
    values = []
    for centre in range(4):
        factor = jnp.ones_like(coordinate)
        for second in range(4):
            if second != centre:
                factor = (
                    factor
                    * (coordinate - node_coords[second])
                    / (node_coords[centre] - node_coords[second])
                )
        values.append(factor)
    return jnp.stack(values, axis=1)


def drag_bins(records, nodal_velocity):
    batch_size = records.shape[0]
    fluid_nodes = nodal_velocity.reshape(batch_size, 3, NODES)
    relax_rate = records[:, 6]
    occupied = records[:, 7]

    def substep(turn_index, carried):
        position, velocity, drag_sum, weight_sum = carried
        basis_one = basis_values(position[:, 0])
        basis_two = basis_values(position[:, 1])
        basis_three = basis_values(position[:, 2])
        weights = (
            basis_one[:, :, None, None, :]
            * basis_two[:, None, :, None, :]
            * basis_three[:, None, None, :, :]
        ).reshape(batch_size, NODES, -1)
        at_particle = jnp.einsum("bcn,bnp->bcp", fluid_nodes, weights, precision=exact_mode)
        change = (relax_rate * occupied)[:, None, :] * (at_particle - velocity)
        velocity = velocity + change
        position = jnp.clip(position + stride_step * occupied[:, None, :] * velocity, -1.0, 1.0)
        drag_sum = drag_sum + jnp.einsum("bnp,bcp->bcn", weights, change, precision=exact_mode)
        weight_sum = weight_sum + jnp.einsum(
            "bnp,bp->bn", weights * weights, occupied, precision=exact_mode
        )
        return (position, velocity, drag_sum, weight_sum)

    start_state = (
        records[:, 0:3],
        records[:, 3:6],
        jnp.zeros((batch_size, 3, NODES), jnp.float32),
        jnp.zeros((batch_size, NODES), jnp.float32),
    )
    position, velocity, drag_sum, weight_sum = lax.fori_loop(0, SUBSTEPS, substep, start_state)
    moved_state = jnp.concatenate([position, velocity], axis=1)
    nodal_sums = jnp.concatenate([drag_sum.reshape(batch_size, 3 * NODES), weight_sum], axis=1)
    return (moved_state, nodal_sums)


def local_update(
    field, viscosity, axial_speed, after_airway, before_airway, after_section, before_section
):
    operator = jnp.asarray(operator_table(), dtype=jnp.float32)
    applied = jnp.einsum("mn,cnse->cmse", operator, field, precision=exact_mode)
    cube = field.reshape((3, 4, 4, 4) + field.shape[2:])
    faces = jnp.zeros_like(cube)
    faces = faces.at[:, 3].add(after_airway - cube[:, 3])
    faces = faces.at[:, 0].add(before_airway - cube[:, 0])
    faces = faces.at[:, :, 3].add(after_section - cube[:, :, 3])
    faces = faces.at[:, :, 0].add(before_section - cube[:, :, 0])
    return (
        field
        + viscosity * applied[:, :NODES]
        - axial_speed * applied[:, NODES:]
        + penalty_weight * faces.reshape(field.shape)
    )


def neighbour_faces(field):
    sec_cells = field.shape[2]
    air_cells = field.shape[3]
    padded = with_halo(field, (("section", 2), ("airway", 3)), 1)
    padded = padded.reshape(3, 4, 4, 4, sec_cells + 2, air_cells + 2)
    after_airway = padded[:, 0, :, :, 1:-1, 2:]
    before_airway = padded[:, 3, :, :, 1:-1, :-2]
    after_section = padded[:, :, 0, :, 2:, 1:-1]
    before_section = padded[:, :, 3, :, :-2, 1:-1]
    return (after_airway, before_airway, after_section, before_section)


def rotate(array, begin):
    doubled = jnp.concatenate([array, array], axis=0)
    return lax.dynamic_slice_in_dim(doubled, begin, array.shape[0], 0)


def send_bins(out_records, out_nodal):
    in_records, in_nodal = (
        lax.all_to_all(out_records, ("airway", "section"), split_axis=0, concat_axis=0, tiled=True),
        lax.all_to_all(out_nodal, ("airway", "section"), split_axis=0, concat_axis=0, tiled=True),
    )
    return (in_records, in_nodal)


def return_bins(back_state, back_sums):
    got_state, got_sums = (
        lax.all_to_all(back_state, ("airway", "section"), split_axis=0, concat_axis=0, tiled=True),
        lax.all_to_all(back_sums, ("airway", "section"), split_axis=0, concat_axis=0, tiled=True),
    )
    return (got_state, got_sums)


def local(
    fluid_velocity,
    viscosity,
    axial_speed,
    fluid_mass,
    positions,
    velocities,
    relax_rates,
    bin_element,
    bin_fill,
):
    sec_cells = fluid_velocity.shape[2]
    air_cells = fluid_velocity.shape[3]
    elements = sec_cells * air_cells
    per_bin = positions.shape[2]
    occupancy = (jnp.arange(per_bin, dtype=jnp.int32)[None, :] < bin_fill[:, None]).astype(
        jnp.float32
    )
    records = jnp.concatenate(
        [positions, velocities, relax_rates[:, None, :], occupancy[:, None, :]], axis=1
    )
    flat_fluid = fluid_velocity.reshape(3 * NODES, elements)
    bin_nodal = jnp.take(flat_fluid, bin_element, axis=1).T
    devices = lax.axis_size("airway") * lax.axis_size("section")
    helpers = devices // 2
    myself = lax.axis_index(("airway", "section"))
    carried_here = jnp.sum((bin_fill[HOME:] > 0).astype(jnp.int32))
    counts = lax.all_gather(carried_here[None], ("airway", "section"), axis=0, tiled=True)
    offsets = jnp.cumsum(counts) - counts
    ranks = jnp.arange(devices, dtype=jnp.int32)
    start_here = jnp.sum(jnp.where(ranks == myself, offsets, 0))
    shift_in = (devices - start_here % devices) % devices
    out_records = rotate(records[HOME:], shift_in)
    out_nodal = rotate(bin_nodal[HOME:], shift_in)
    in_records, in_nodal = send_bins(out_records, out_nodal)
    delta = (myself - offsets) % devices
    arrived = delta < counts
    target = (offsets + delta) // devices
    order_key = jnp.where(arrived, target, helpers + ranks)
    picked = jnp.argsort(order_key)[:helpers]
    batch_records = jnp.concatenate([records[:HOME], jnp.take(in_records, picked, axis=0)], axis=0)
    batch_nodal = jnp.concatenate([bin_nodal[:HOME], jnp.take(in_nodal, picked, axis=0)], axis=0)
    moved_state, nodal_sums = drag_bins(batch_records, batch_nodal)
    back_index = jnp.clip(target, 0, helpers - 1)
    arrived_float = arrived.astype(jnp.float32)
    back_state = jnp.take(moved_state[HOME:], back_index, axis=0) * arrived_float[:, None, None]
    back_sums = jnp.take(nodal_sums[HOME:], back_index, axis=0) * arrived_float[:, None]
    got_state, got_sums = return_bins(back_state, back_sums)
    unroll = start_here % devices
    over_state = rotate(got_state, unroll)
    over_sums = rotate(got_sums, unroll)
    former_state = jnp.concatenate([positions[HOME:], velocities[HOME:]], axis=1)
    slot_used = (bin_fill[HOME:] > 0)[:, None, None]
    over_state = jnp.where(slot_used, over_state, former_state)
    particles_out = jnp.concatenate([moved_state[:HOME], over_state], axis=0)
    all_sums = jnp.concatenate([nodal_sums[:HOME], over_sums], axis=0)
    one_hot = (bin_element[:, None] == jnp.arange(elements, dtype=jnp.int32)[None, :]).astype(
        jnp.float32
    )
    deposited = lax.dot_general(all_sums, one_hot, (((0,), (0,)), ((), ())), precision=exact_mode)
    drag_part = deposited[: 3 * NODES].reshape(3, NODES, sec_cells, air_cells)
    weight_part = deposited[3 * NODES :].reshape(NODES, sec_cells, air_cells)
    field = fluid_velocity - drag_part / (fluid_mass[None, None] + weight_part[None])
    for pass_index in range(PASSES):
        after_airway, before_airway, after_section, before_section = neighbour_faces(field)
        field = local_update(
            field,
            viscosity,
            axial_speed,
            after_airway,
            before_airway,
            after_section,
            before_section,
        )
    return (field, particles_out)


def solution(mesh):
    return jax.shard_map(
        local,
        mesh=mesh,
        in_specs=(
            P(None, None, "section", "airway"),
            P("section", "airway"),
            P("section", "airway"),
            P("section", "airway"),
            P(("airway", "section"), None, None),
            P(("airway", "section"), None, None),
            P(("airway", "section"), None),
            P(("airway", "section")),
            P(("airway", "section")),
        ),
        out_specs=(P(None, None, "section", "airway"), P(("airway", "section"), None, None)),
        check_vma=False,
    )
```

profile of v0, /device:TPU:0, one launch (start us, length us, event | category | flops | bytes accessed | tf_op | source)
XLA Modules:
  0.0 666.0 jit_solution(9321328653382917952)
XLA Ops:
  4.1 68.1 %all-reduce.4 = s32[128]{0:T(128)S(1)} all-reduce(s32[128]{0:T(128)S(1)} %dynamic-update-slice.48), channel_id=1, replica_groups=mesh['airway'=8,'section'=16] {'airway','section'}, use_global_device_ids=true, to_apply=%add.4 | all-reduce | flops 128 | bytes 1024
  82.3 4.8 all-to-all-start.1
  91.8 4.9 all-to-all-done.1
  96.7 4.9 all-to-all-start
  102.7 12.5 %all-to-all-done = f32[128,8,128]{2,1,0:T(8,128)S(1)} async-done(((f32[128,8,128]{2,1,0:T(8,128)}), f32[128,8,128]{2,1,0:T(8,128)S(1)}, u32[]{:S(2)}, u32[]{:S(2)}) %all-to-all-start) | async-done | bytes 524320 | tf_op jit(solution)/shard_map/all_to_all | solution.py:160
  116.4 313.8 %while.36 = (s32[]{:T(128)}, f32[128,3,128]{2,0,1:T(8,128)S(1)}, f32[128,3,128]{2,0,1:T(8,128)S(1)}, f32[128,3,64]{2,1,0:T(4,128)S(1)}, f32[128,64]{1,0:T(8,128)...) while((s32[]{:T(128)}, f32[128,3,128]{2,0,1:T(8,128)S(1)}, ...), condition=%wide.region_5.6_spmd.clone, body=%wide.region_4.5_spmd.clone.sunk | while | flops 92585984 | bytes 26509428 | solution.py:116
  119.1 6.6 fusion.92
  125.7 3.7 fusion.91
  129.5 6.7 %convolution_add_fusion.2 = f32[128,3,64]{2,1,0:T(4,128)S(1)} fusion(f32[128,3,128]{2,1,0:T(4,128)S(1)} %get-tuple-element.616, f32[128,64,128]{2,1,0:T(8,128)S(1)} %bitcast.131, f32[128,3,64]{2,1,0:T(4,128)S(1)} %get-tuple-element.631, pred[]{:T(512)S(6)} %compare.105), kind=kOutput, calls=%fused_computation.8.clone.1 | convolution fusion | flops 37797888 | bytes 4587521 | tf_op jit(solution)/shard_map/while/body/eval_jaxpr/bnp,bcp->bcn/dot_general | solution.py:104
  138.7 6.6 fusion.92
  145.3 3.7 fusion.91
  149.0 6.7 %convolution_add_fusion.2 = f32[128,3,64]{2,1,0:T(4,128)S(1)} fusion(f32[128,3,128]{2,1,0:T(4,128)S(1)} %get-tuple-element.616, f32[128,64,128]{2,1,0:T(8,128)S(1)} %bitcast.131, f32[128,3,64]{2,1,0:T(4,128)S(1)} %get-tuple-element.631, pred[]{:T(512)S(6)} %compare.105), kind=kOutput, calls=%fused_computation.8.clone.1 | convolution fusion | flops 37797888 | bytes 4587521 | tf_op jit(solution)/shard_map/while/body/eval_jaxpr/bnp,bcp->bcn/dot_general | solution.py:104
  158.2 6.6 fusion.92
  164.8 3.7 fusion.91
  168.6 6.7 %convolution_add_fusion.2 = f32[128,3,64]{2,1,0:T(4,128)S(1)} fusion(f32[128,3,128]{2,1,0:T(4,128)S(1)} %get-tuple-element.616, f32[128,64,128]{2,1,0:T(8,128)S(1)} %bitcast.131, f32[128,3,64]{2,1,0:T(4,128)S(1)} %get-tuple-element.631, pred[]{:T(512)S(6)} %compare.105), kind=kOutput, calls=%fused_computation.8.clone.1 | convolution fusion | flops 37797888 | bytes 4587521 | tf_op jit(solution)/shard_map/while/body/eval_jaxpr/bnp,bcp->bcn/dot_general | solution.py:104
  177.8 6.6 fusion.92
  184.4 3.7 fusion.91
  188.2 6.7 %convolution_add_fusion.2 = f32[128,3,64]{2,1,0:T(4,128)S(1)} fusion(f32[128,3,128]{2,1,0:T(4,128)S(1)} %get-tuple-element.616, f32[128,64,128]{2,1,0:T(8,128)S(1)} %bitcast.131, f32[128,3,64]{2,1,0:T(4,128)S(1)} %get-tuple-element.631, pred[]{:T(512)S(6)} %compare.105), kind=kOutput, calls=%fused_computation.8.clone.1 | convolution fusion | flops 37797888 | bytes 4587521 | tf_op jit(solution)/shard_map/while/body/eval_jaxpr/bnp,bcp->bcn/dot_general | solution.py:104
  197.4 6.6 fusion.92
  204.0 3.7 fusion.91
  207.7 6.7 %convolution_add_fusion.2 = f32[128,3,64]{2,1,0:T(4,128)S(1)} fusion(f32[128,3,128]{2,1,0:T(4,128)S(1)} %get-tuple-element.616, f32[128,64,128]{2,1,0:T(8,128)S(1)} %bitcast.131, f32[128,3,64]{2,1,0:T(4,128)S(1)} %get-tuple-element.631, pred[]{:T(512)S(6)} %compare.105), kind=kOutput, calls=%fused_computation.8.clone.1 | convolution fusion | flops 37797888 | bytes 4587521 | tf_op jit(solution)/shard_map/while/body/eval_jaxpr/bnp,bcp->bcn/dot_general | solution.py:104
  216.9 6.6 fusion.92
  223.6 3.7 fusion.91
  227.3 6.7 %convolution_add_fusion.2 = f32[128,3,64]{2,1,0:T(4,128)S(1)} fusion(f32[128,3,128]{2,1,0:T(4,128)S(1)} %get-tuple-element.616, f32[128,64,128]{2,1,0:T(8,128)S(1)} %bitcast.131, f32[128,3,64]{2,1,0:T(4,128)S(1)} %get-tuple-element.631, pred[]{:T(512)S(6)} %compare.105), kind=kOutput, calls=%fused_computation.8.clone.1 | convolution fusion | flops 37797888 | bytes 4587521 | tf_op jit(solution)/shard_map/while/body/eval_jaxpr/bnp,bcp->bcn/dot_general | solution.py:104
  236.5 6.6 fusion.92
  246.9 6.7 %convolution_add_fusion.2 = f32[128,3,64]{2,1,0:T(4,128)S(1)} fusion(f32[128,3,128]{2,1,0:T(4,128)S(1)} %get-tuple-element.616, f32[128,64,128]{2,1,0:T(8,128)S(1)} %bitcast.131, f32[128,3,64]{2,1,0:T(4,128)S(1)} %get-tuple-element.631, pred[]{:T(512)S(6)} %compare.105), kind=kOutput, calls=%fused_computation.8.clone.1 | convolution fusion | flops 37797888 | bytes 4587521 | tf_op jit(solution)/shard_map/while/body/eval_jaxpr/bnp,bcp->bcn/dot_general | solution.py:104
  256.1 6.6 fusion.92
  266.5 6.7 %convolution_add_fusion.2 = f32[128,3,64]{2,1,0:T(4,128)S(1)} fusion(f32[128,3,128]{2,1,0:T(4,128)S(1)} %get-tuple-element.616, f32[128,64,128]{2,1,0:T(8,128)S(1)} %bitcast.131, f32[128,3,64]{2,1,0:T(4,128)S(1)} %get-tuple-element.631, pred[]{:T(512)S(6)} %compare.105), kind=kOutput, calls=%fused_computation.8.clone.1 | convolution fusion | flops 37797888 | bytes 4587521 | tf_op jit(solution)/shard_map/while/body/eval_jaxpr/bnp,bcp->bcn/dot_general | solution.py:104
  275.7 6.6 fusion.92
  286.0 6.7 %convolution_add_fusion.2 = f32[128,3,64]{2,1,0:T(4,128)S(1)} fusion(f32[128,3,128]{2,1,0:T(4,128)S(1)} %get-tuple-element.616, f32[128,64,128]{2,1,0:T(8,128)S(1)} %bitcast.131, f32[128,3,64]{2,1,0:T(4,128)S(1)} %get-tuple-element.631, pred[]{:T(512)S(6)} %compare.105), kind=kOutput, calls=%fused_computation.8.clone.1 | convolution fusion | flops 37797888 | bytes 4587521 | tf_op jit(solution)/shard_map/while/body/eval_jaxpr/bnp,bcp->bcn/dot_general | solution.py:104
  295.2 6.6 fusion.92
  305.6 6.7 %convolution_add_fusion.2 = f32[128,3,64]{2,1,0:T(4,128)S(1)} fusion(f32[128,3,128]{2,1,0:T(4,128)S(1)} %get-tuple-element.616, f32[128,64,128]{2,1,0:T(8,128)S(1)} %bitcast.131, f32[128,3,64]{2,1,0:T(4,128)S(1)} %get-tuple-element.631, pred[]{:T(512)S(6)} %compare.105), kind=kOutput, calls=%fused_computation.8.clone.1 | convolution fusion | flops 37797888 | bytes 4587521 | tf_op jit(solution)/shard_map/while/body/eval_jaxpr/bnp,bcp->bcn/dot_general | solution.py:104
  314.8 6.6 fusion.92
  325.2 6.7 %convolution_add_fusion.2 = f32[128,3,64]{2,1,0:T(4,128)S(1)} fusion(f32[128,3,128]{2,1,0:T(4,128)S(1)} %get-tuple-element.616, f32[128,64,128]{2,1,0:T(8,128)S(1)} %bitcast.131, f32[128,3,64]{2,1,0:T(4,128)S(1)} %get-tuple-element.631, pred[]{:T(512)S(6)} %compare.105), kind=kOutput, calls=%fused_computation.8.clone.1 | convolution fusion | flops 37797888 | bytes 4587521 | tf_op jit(solution)/shard_map/while/body/eval_jaxpr/bnp,bcp->bcn/dot_general | solution.py:104
  334.4 6.6 fusion.92
  344.7 6.7 %convolution_add_fusion.2 = f32[128,3,64]{2,1,0:T(4,128)S(1)} fusion(f32[128,3,128]{2,1,0:T(4,128)S(1)} %get-tuple-element.616, f32[128,64,128]{2,1,0:T(8,128)S(1)} %bitcast.131, f32[128,3,64]{2,1,0:T(4,128)S(1)} %get-tuple-element.631, pred[]{:T(512)S(6)} %compare.105), kind=kOutput, calls=%fused_computation.8.clone.1 | convolution fusion | flops 37797888 | bytes 4587521 | tf_op jit(solution)/shard_map/while/body/eval_jaxpr/bnp,bcp->bcn/dot_general | solution.py:104
  353.9 6.6 fusion.92
  360.6 3.7 fusion.91
  364.3 6.7 %convolution_add_fusion.2 = f32[128,3,64]{2,1,0:T(4,128)S(1)} fusion(f32[128,3,128]{2,1,0:T(4,128)S(1)} %get-tuple-element.616, f32[128,64,128]{2,1,0:T(8,128)S(1)} %bitcast.131, f32[128,3,64]{2,1,0:T(4,128)S(1)} %get-tuple-element.631, pred[]{:T(512)S(6)} %compare.105), kind=kOutput, calls=%fused_computation.8.clone.1 | convolution fusion | flops 37797888 | bytes 4587521 | tf_op jit(solution)/shard_map/while/body/eval_jaxpr/bnp,bcp->bcn/dot_general | solution.py:104
  373.5 6.6 fusion.92
  383.9 6.7 %convolution_add_fusion.2 = f32[128,3,64]{2,1,0:T(4,128)S(1)} fusion(f32[128,3,128]{2,1,0:T(4,128)S(1)} %get-tuple-element.616, f32[128,64,128]{2,1,0:T(8,128)S(1)} %bitcast.131, f32[128,3,64]{2,1,0:T(4,128)S(1)} %get-tuple-element.631, pred[]{:T(512)S(6)} %compare.105), kind=kOutput, calls=%fused_computation.8.clone.1 | convolution fusion | flops 37797888 | bytes 4587521 | tf_op jit(solution)/shard_map/while/body/eval_jaxpr/bnp,bcp->bcn/dot_general | solution.py:104
  393.1 6.6 fusion.92
  403.5 6.7 %convolution_add_fusion.2 = f32[128,3,64]{2,1,0:T(4,128)S(1)} fusion(f32[128,3,128]{2,1,0:T(4,128)S(1)} %get-tuple-element.616, f32[128,64,128]{2,1,0:T(8,128)S(1)} %bitcast.131, f32[128,3,64]{2,1,0:T(4,128)S(1)} %get-tuple-element.631, pred[]{:T(512)S(6)} %compare.105), kind=kOutput, calls=%fused_computation.8.clone.1 | convolution fusion | flops 37797888 | bytes 4587521 | tf_op jit(solution)/shard_map/while/body/eval_jaxpr/bnp,bcp->bcn/dot_general | solution.py:104
  412.6 6.6 fusion.92
  419.3 3.7 fusion.91
  423.0 6.7 %convolution_add_fusion.2 = f32[128,3,64]{2,1,0:T(4,128)S(1)} fusion(f32[128,3,128]{2,1,0:T(4,128)S(1)} %get-tuple-element.616, f32[128,64,128]{2,1,0:T(8,128)S(1)} %bitcast.131, f32[128,3,64]{2,1,0:T(4,128)S(1)} %get-tuple-element.631, pred[]{:T(512)S(6)} %compare.105), kind=kOutput, calls=%fused_computation.8.clone.1 | convolution fusion | flops 37797888 | bytes 4587521 | tf_op jit(solution)/shard_map/while/body/eval_jaxpr/bnp,bcp->bcn/dot_general | solution.py:104
  432.2 4.6 all-to-all-start.2
  436.8 9.6 %all-to-all-done.2 = f32[128,1,256]{2,1,0:T(1,128)S(1)} async-done(((f32[128,1,256]{2,1,0:T(1,128)}), f32[128,1,256]{2,1,0:T(1,128)S(1)}, u32[]{:S(2)}, u32[]{:S(2)}) %all-to-all-start.2) | async-done | bytes 131104 | tf_op jit(solution)/shard_map/all_to_all | solution.py:169
  459.3 4.1 collective-permute-done.1
  473.0 4.3 convolution_bitcast_fusion.4
  482.0 4.3 pad_maximum_fusion.3
  486.3 4.7 reshape.916
  526.7 4.3 convolution_bitcast_fusion.3
  535.6 4.2 pad_maximum_fusion.4
  539.8 4.7 reshape.918
  556.1 5.6 collective-permute-start.8
  564.2 9.9 %all-to-all-start.3 = ((f32[128,6,128]{2,1,0:T(8,128)}), f32[128,6,128]{2,1,0:T(8,128)}, u32[]{:S(2)}, u32[]{:S(2)}) async-start(f32[128,6,128]{2,1,0:T(8,128)} %select_multiply_fusion), calls=%async_computation.3 | async-start | bytes 1048576 | tf_op jit(solution)/shard_map/all_to_all | solution.py:168
  582.8 5.1 convolution_bitcast_fusion.2
  592.5 4.2 pad_maximum_fusion.5
  596.7 4.7 reshape.920
  621.1 4.1 collective-permute-done.13
  633.2 5.1 convolution_bitcast_fusion.1
  643.0 4.2 pad_maximum_fusion.6
  647.1 4.8 reshape.922
  (450 shorter events, 229.3 us)
Async XLA Ops:
  72.7 358.6 %copy-start.33 = (pred[128]{0:T(512)(128)(4,1)}, pred[128]{0:T(512)(128)(4,1)S(1)}, u32[]{:S(2)}) copy-start(pred[128]{0:T(512)(128)(4,1)S(1)} %get-tuple-element.481) | copy-start | bytes 388
  80.3 6.8 %copy-start.38 = (s32[192]{0:T(256)S(1)}, s32[192]{0:T(256)}, u32[]{:S(2)}) copy-start(s32[192]{0:T(256)} %param.55) | copy-start | bytes 2308
  80.4 9.6 %copy-start.27 = (f32[192,3,128]{2,0,1:T(8,128)S(1)}, f32[192,3,128]{2,0,1:T(8,128)}, u32[]{:S(2)}) copy-start(f32[192,3,128]{2,0,1:T(8,128)} %param.51) | copy-start | bytes 884740
  81.2 9.0 %copy-start.28 = (f32[192,3,128]{2,0,1:T(8,128)S(1)}, f32[192,3,128]{2,0,1:T(8,128)}, u32[]{:S(2)}) copy-start(f32[192,3,128]{2,0,1:T(8,128)} %param.52) | copy-start | bytes 884740
  81.2 9.2 %copy-start.26 = (f32[192,128]{1,0:T(8,128)S(1)}, f32[192,128]{1,0:T(8,128)}, u32[]{:S(2)}) copy-start(f32[192,128]{1,0:T(8,128)} %param.53) | copy-start | bytes 294916
  81.4 9.4 %copy-start.9 = (f32[192,192]{1,0:T(8,128)}, f32[192,192]{1,0:T(8,128)S(1)}, u32[]{:S(2)}) copy-start(f32[192,192]{1,0:T(8,128)S(1)} %broadcast_select_fusion.1) | copy-start | bytes 442372
  82.3 14.4 %all-to-all-start.1 = ((f32[128,1,192]{2,1,0:T(1,128)}), f32[128,1,192]{2,1,0:T(1,128)S(1)}, u32[]{:S(2)}, u32[]{:S(2)}) async-start(f32[128,1,192]{2,1,0:T(1,128)} %copy.127), calls=%async_computation.1 | async-start | bytes 262144 | tf_op jit(solution)/shard_map/all_to_all | solution.py:161
  90.2 25.8 %copy-start.5 = (f32[192,3,128]{2,1,0:T(4,128)}, f32[192,3,128]{2,1,0:T(4,128)S(1)}, u32[]{:S(2)}) copy-start(f32[192,3,128]{2,1,0:T(4,128)S(1)} %copy.122) | copy-start | bytes 884740
  90.4 25.6 %copy-start.4 = (f32[192,3,128]{2,1,0:T(4,128)}, f32[192,3,128]{2,1,0:T(4,128)S(1)}, u32[]{:S(2)}) copy-start(f32[192,3,128]{2,1,0:T(4,128)S(1)} %copy.123) | copy-start | bytes 884740
  91.8 10.6 %slice-start.2 = ((f32[192,192]{1,0:T(8,128)}), f32[64,192]{1,0:T(8,128)S(1)}, s32[]{:S(2)}) async-start(f32[192,192]{1,0:T(8,128)} %copy-done.9), calls=%async_computation.6 | async-start | bytes 131072 | tf_op jit(solution)/shard_map/slice | solution.py:215
  91.8 338.7 %copy-start.32 = (s32[1024]{0:T(1024)}, s32[1024]{0:T(1024)S(1)}, u32[]{:S(2)}) copy-start(s32[1024]{0:T(1024)S(1)} %pad_clamp_fusion) | copy-start | bytes 12292
  96.7 18.5 %all-to-all-start = ((f32[128,8,128]{2,1,0:T(8,128)}), f32[128,8,128]{2,1,0:T(8,128)S(1)}, u32[]{:S(2)}, u32[]{:S(2)}) async-start(f32[128,8,128]{2,1,0:T(8,128)} %fusion.21), calls=%async_computation | async-start | bytes 1048576 | tf_op jit(solution)/shard_map/all_to_all | solution.py:160
  101.6 329.6 %copy-start.36 = (f32[128]{0:T(128)}, f32[128]{0:T(128)S(1)}, u32[]{:S(2)}) copy-start(f32[128]{0:T(128)S(1)} %compare_convert_fusion.1) | copy-start | bytes 1540
  430.3 16.2 %copy-start.35 = (s32[192]{0:T(256)S(1)}, s32[192]{0:T(256)}, u32[]{:S(2)}) copy-start(s32[192]{0:T(256)} %param.54) | copy-start | bytes 2308
  432.2 14.2 %all-to-all-start.2 = ((f32[128,1,256]{2,1,0:T(1,128)}), f32[128,1,256]{2,1,0:T(1,128)S(1)}, u32[]{:S(2)}, u32[]{:S(2)}) async-start(f32[128,1,256]{2,1,0:T(1,128)} %copy.138), calls=%async_computation.2 | async-start | bytes 262144 | tf_op jit(solution)/shard_map/all_to_all | solution.py:169
  447.7 1.3 copy-start
  449.0 1.0 slice-start
  449.0 1.2 copy-start.31
  450.0 1.4 copy-start.3
  452.4 6.9 %collective-permute-start = (f32[3,64,1,256]{3,1,2,0:T(8,128)S(1)}, f32[3,64,1,256]{3,1,2,0:T(8,128)S(1)}, u32[]{:S(2)}, u32[]{:S(2)}) collective-permute-start(f32[3,64,1,256]{3,1,2,0:T(8,128)S(1)} %get-tuple-element.516), channel_id=1, source_target_pairs={{0,1},{1,2},{2,3},{3,4},{4,5},{5,6},{6,7},{7,8},{8,9},{9,10},{10,1... | collective-permute-start | bytes 589832 | tf_op jit(solution)/shard_map/ppermute | solution.py:27
  455.0 8.5 %collective-permute-start.1 = (f32[3,64,1,256]{3,1,2,0:T(8,128)S(1)}, f32[3,64,1,256]{3,1,2,0:T(8,128)S(1)}, u32[]{:S(2)}, u32[]{:S(2)}) collective-permute-start(f32[3,64,1,256]{3,1,2,0:T(8,128)S(1)} %get-tuple-element.517), channel_id=1, source_target_pairs={{1,0},{2,1},{3,2},{4,3},{5,4},{6,5},{7,6},{8,7},{9,8},{10,9},{11,1... | collective-permute-start | bytes 589832 | tf_op jit(solution)/shard_map/ppermute | solution.py:29
  459.3 4.1 copy-start.22
  463.4 0.7 copy-start.23
  465.6 7.4 %copy-start.24 = (f32[128,64,1,1]{0,1,3,2:T(8,128)S(1)}, f32[128,64,1,1]{0,1,3,2:T(8,128)}, u32[]{:S(2)}) copy-start(f32[128,64,1,1]{0,1,3,2:T(8,128)} %constant.652) | copy-start | bytes 98308
  468.1 11.8 %collective-permute-start.3 = (f32[3,64,10,1]{1,3,2,0:T(1,128)S(1)}, f32[3,64,10,1]{1,3,2,0:T(1,128)}, u32[]{:S(2)}, u32[]{:S(2)}) collective-permute-start(f32[3,64,10,1]{1,3,2,0:T(1,128)S(1)} %copy.143), channel_id=1, source_target_pairs={{16,0},{32,16},{48,32},{64,48},{80,64},{96,80},{112,96},{17,1},{33... | collective-permute-start | bytes 23048 | tf_op jit(solution)/shard_map/ppermute | solution.py:29
  469.4 8.4 %collective-permute-start.2 = (f32[3,64,10,1]{1,3,2,0:T(1,128)}, f32[3,64,10,1]{1,3,2,0:T(1,128)}, u32[]{:S(2)}, u32[]{:S(2)}) collective-permute-start(f32[3,64,10,1]{1,3,2,0:T(1,128)} %copy.142), channel_id=1, source_target_pairs={{0,16},{16,32},{32,48},{48,64},{64,80},{80,96},{96,112},{1,17},{17... | collective-permute-start | bytes 23048 | tf_op jit(solution)/shard_map/ppermute | solution.py:27
  477.8 13.2 %copy-start.1 = (f32[3,4,4,4,8,256]{5,3,2,1,4,0:T(4,128)}, f32[3,4,4,4,8,256]{5,3,2,1,4,0:T(4,128)S(1)}, u32[]{:S(2)}) copy-start(f32[3,4,4,4,8,256]{5,3,2,1,4,0:T(4,128)S(1)} %reshape.917) | copy-start | bytes 4718596
  492.3 1.4 copy-start.2
  500.1 2.8 copy-start.29
  500.1 2.8 copy-start.30
  503.0 6.8 %copy-start.39 = (s32[192]{0:T(256)S(1)}, s32[192]{0:T(256)}, u32[]{:S(2)}) copy-start(s32[192]{0:T(256)} %param.55) | copy-start | bytes 2308
  503.0 7.3 %copy-start.6 = (f32[192,3,128]{2,1,0:T(4,128)S(1)}, f32[192,3,128]{2,1,0:T(4,128)}, u32[]{:S(2)}) copy-start(f32[192,3,128]{2,1,0:T(4,128)} %copy-done.5) | copy-start | bytes 884740
  506.1 7.7 %collective-permute-start.4 = (f32[3,64,1,256]{3,1,2,0:T(8,128)S(1)}, f32[3,64,1,256]{3,1,2,0:T(8,128)S(1)}, u32[]{:S(2)}, u32[]{:S(2)}) collective-permute-start(f32[3,64,1,256]{3,1,2,0:T(8,128)S(1)} %get-tuple-element.514), channel_id=1, source_target_pairs={{0,1},{1,2},{2,3},{3,4},{4,5},{5,6},{6,7},{7,8},{8,9},{9,10},{10,1... | collective-permute-start | bytes 589832 | tf_op jit(solution)/shard_map/ppermute | solution.py:27
  508.4 8.1 %collective-permute-start.5 = (f32[3,64,1,256]{3,1,2,0:T(8,128)S(1)}, f32[3,64,1,256]{3,1,2,0:T(8,128)S(1)}, u32[]{:S(2)}, u32[]{:S(2)}) collective-permute-start(f32[3,64,1,256]{3,1,2,0:T(8,128)S(1)} %get-tuple-element.515), channel_id=1, source_target_pairs={{1,0},{2,1},{3,2},{4,3},{5,4},{6,5},{7,6},{8,7},{9,8},{10,9},{11,1... | collective-permute-start | bytes 589832 | tf_op jit(solution)/shard_map/ppermute | solution.py:29
  513.8 2.7 copy-start.10
  516.5 0.7 copy-start.14
  518.6 8.0 %copy-start.25 = (f32[128,64,1,1]{0,1,3,2:T(8,128)S(1)}, f32[128,64,1,1]{0,1,3,2:T(8,128)}, u32[]{:S(2)}) copy-start(f32[128,64,1,1]{0,1,3,2:T(8,128)} %constant.652) | copy-start | bytes 98308
  521.8 11.8 %collective-permute-start.7 = (f32[3,64,10,1]{1,3,2,0:T(1,128)}, f32[3,64,10,1]{1,3,2,0:T(1,128)}, u32[]{:S(2)}, u32[]{:S(2)}) collective-permute-start(f32[3,64,10,1]{1,3,2,0:T(1,128)} %copy.147), channel_id=1, source_target_pairs={{16,0},{32,16},{48,32},{64,48},{80,64},{96,80},{112,96},{17,1},{33... | collective-permute-start | bytes 23048 | tf_op jit(solution)/shard_map/ppermute | solution.py:29
  523.0 8.4 %collective-permute-start.6 = (f32[3,64,10,1]{1,3,2,0:T(1,128)}, f32[3,64,10,1]{1,3,2,0:T(1,128)}, u32[]{:S(2)}, u32[]{:S(2)}) collective-permute-start(f32[3,64,10,1]{1,3,2,0:T(1,128)} %copy.146), channel_id=1, source_target_pairs={{0,16},{16,32},{32,48},{48,64},{64,80},{80,96},{96,112},{1,17},{17... | collective-permute-start | bytes 23048 | tf_op jit(solution)/shard_map/ppermute | solution.py:27
  531.4 4.2 copy-start.11
  531.4 4.2 copy-start.15
  553.0 10.0 %copy-start.7 = (f32[128,6,128]{2,1,0:T(8,128)S(1)}, f32[128,6,128]{2,1,0:T(8,128)}, u32[]{:S(2)}) copy-start(f32[128,6,128]{2,1,0:T(8,128)} %gather_fusion.4) | copy-start | bytes 1179652
  553.0 10.0 %copy-start.34 = (pred[128]{0:T(512)(128)(4,1)S(1)}, pred[128]{0:T(512)(128)(4,1)}, u32[]{:S(2)}) copy-start(pred[128]{0:T(512)(128)(4,1)} %copy-done.33) | copy-start | bytes 388
  553.0 10.0 %copy-start.37 = (f32[128]{0:T(128)S(1)}, f32[128]{0:T(128)}, u32[]{:S(2)}) copy-start(f32[128]{0:T(128)} %copy-done.36) | copy-start | bytes 1540
  556.1 18.0 %collective-permute-start.8 = (f32[3,64,1,256]{3,1,2,0:T(8,128)S(1)}, f32[3,64,1,256]{3,1,2,0:T(8,128)S(1)}, u32[]{:S(2)}, u32[]{:S(2)}) collective-permute-start(f32[3,64,1,256]{3,1,2,0:T(8,128)S(1)} %get-tuple-element.512), channel_id=1, source_target_pairs={{0,1},{1,2},{2,3},{3,4},{4,5},{5,6},{6,7},{7,8},{8,9},{9,10},{10,1... | collective-permute-start | bytes 589832 | tf_op jit(solution)/shard_map/ppermute | solution.py:27
  561.8 12.4 %collective-permute-start.9 = (f32[3,64,1,256]{3,1,2,0:T(8,128)S(1)}, f32[3,64,1,256]{3,1,2,0:T(8,128)S(1)}, u32[]{:S(2)}, u32[]{:S(2)}) collective-permute-start(f32[3,64,1,256]{3,1,2,0:T(8,128)S(1)} %get-tuple-element.513), channel_id=1, source_target_pairs={{1,0},{2,1},{3,2},{4,3},{5,4},{6,5},{7,6},{8,7},{9,8},{10,9},{11,1... | collective-permute-start | bytes 589832 | tf_op jit(solution)/shard_map/ppermute | solution.py:29
  564.2 53.1 %all-to-all-start.3 = ((f32[128,6,128]{2,1,0:T(8,128)}), f32[128,6,128]{2,1,0:T(8,128)}, u32[]{:S(2)}, u32[]{:S(2)}) async-start(f32[128,6,128]{2,1,0:T(8,128)} %select_multiply_fusion), calls=%async_computation.3 | async-start | bytes 1048576 | tf_op jit(solution)/shard_map/all_to_all | solution.py:168
  574.1 0.7 copy-start.18
  574.8 0.7 copy-start.20
  577.9 12.6 %collective-permute-start.11 = (f32[3,64,10,1]{1,3,2,0:T(1,128)}, f32[3,64,10,1]{1,3,2,0:T(1,128)}, u32[]{:S(2)}, u32[]{:S(2)}) collective-permute-start(f32[3,64,10,1]{1,3,2,0:T(1,128)} %copy.151), channel_id=1, source_target_pairs={{16,0},{32,16},{48,32},{64,48},{80,64},{96,80},{112,96},{17,1},{33... | collective-permute-start | bytes 23048 | tf_op jit(solution)/shard_map/ppermute | solution.py:29
  579.2 9.2 %collective-permute-start.10 = (f32[3,64,10,1]{1,3,2,0:T(1,128)}, f32[3,64,10,1]{1,3,2,0:T(1,128)}, u32[]{:S(2)}, u32[]{:S(2)}) collective-permute-start(f32[3,64,10,1]{1,3,2,0:T(1,128)} %copy.150), channel_id=1, source_target_pairs={{0,16},{16,32},{32,48},{48,64},{64,80},{80,96},{96,112},{1,17},{17... | collective-permute-start | bytes 23048 | tf_op jit(solution)/shard_map/ppermute | solution.py:27
  588.3 4.2 copy-start.19
  588.4 4.2 copy-start.21
  610.0 7.4 %slice-start.1 = ((f32[192,3,128]{2,1,0:T(4,128)}), f32[128,3,128]{2,1,0:T(4,128)S(1)}, s32[]{:S(2)}) async-start(f32[192,3,128]{2,1,0:T(4,128)} %copy-done.4), calls=%async_computation.5 | async-start | bytes 524288 | tf_op jit(solution)/shard_map/slice | solution.py:225
  613.0 5.7 copy-start.8
  613.1 8.0 %collective-permute-start.12 = (f32[3,64,1,256]{3,1,2,0:T(8,128)S(1)}, f32[3,64,1,256]{3,1,2,0:T(8,128)S(1)}, u32[]{:S(2)}, u32[]{:S(2)}) collective-permute-start(f32[3,64,1,256]{3,1,2,0:T(8,128)S(1)} %get-tuple-element.510), channel_id=1, source_target_pairs={{0,1},{1,2},{2,3},{3,4},{4,5},{5,6},{6,7},{7,8},{8,9},{9,10},{10,1... | collective-permute-start | bytes 589832 | tf_op jit(solution)/shard_map/ppermute | solution.py:27
  616.0 9.2 %collective-permute-start.13 = (f32[3,64,1,256]{3,1,2,0:T(8,128)S(1)}, f32[3,64,1,256]{3,1,2,0:T(8,128)S(1)}, u32[]{:S(2)}, u32[]{:S(2)}) collective-permute-start(f32[3,64,1,256]{3,1,2,0:T(8,128)S(1)} %get-tuple-element.511), channel_id=1, source_target_pairs={{1,0},{2,1},{3,2},{4,3},{5,4},{6,5},{7,6},{8,7},{9,8},{10,9},{11,1... | collective-permute-start | bytes 589832 | tf_op jit(solution)/shard_map/ppermute | solution.py:29
  621.1 4.1 copy-start.12
  625.3 0.7 copy-start.16
  628.3 12.6 %collective-permute-start.15 = (f32[3,64,10,1]{1,3,2,0:T(1,128)}, f32[3,64,10,1]{1,3,2,0:T(1,128)}, u32[]{:S(2)}, u32[]{:S(2)}) collective-permute-start(f32[3,64,10,1]{1,3,2,0:T(1,128)} %copy.155), channel_id=1, source_target_pairs={{16,0},{32,16},{48,32},{64,48},{80,64},{96,80},{112,96},{17,1},{33... | collective-permute-start | bytes 23048 | tf_op jit(solution)/shard_map/ppermute | solution.py:29
  629.6 9.2 %collective-permute-start.14 = (f32[3,64,10,1]{1,3,2,0:T(1,128)}, f32[3,64,10,1]{1,3,2,0:T(1,128)}, u32[]{:S(2)}, u32[]{:S(2)}) collective-permute-start(f32[3,64,10,1]{1,3,2,0:T(1,128)} %copy.154), channel_id=1, source_target_pairs={{0,16},{16,32},{32,48},{48,64},{64,80},{80,96},{96,112},{1,17},{17... | collective-permute-start | bytes 23048 | tf_op jit(solution)/shard_map/ppermute | solution.py:27
  638.8 4.2 copy-start.13
  638.8 4.2 copy-start.17
where the time goes:
time: 677 us; the launch traced here: 666 us
  matrix products  292 us (43%)
  other arithmetic  100 us (15%)
  local copies, waits for them, and re-layouts  93.7 us (14%)
  blocking collectives  68.1 us (10%)
  starting transfers between devices  62.5 us (9%)
  waiting for transfers between devices  42.3 us (6%)
    dot_general x16, matrix products, substep(): jnp.einsum('bnp,bcp->bcn', weights, change, precision=exact_mode)  107 us
    dot_general x16, matrix products, substep(): jnp.einsum('bnp,bp->bn', weights * weights, occupied, precision=exact_mode)  105 us
    unnamed x1, blocking collectives  68.1 us
    dot_general x16, matrix products, substep(): jnp.einsum('bcn,bnp->bcp', fluid_nodes, weights, precision=exact_mode)  59.9 us
    ppermute x8, starting transfers between devices, with_halo(): lax.ppermute(tail, axis, [(i, (i + 1) % count) for i in range(ends)])  27.9 us
    mul x32, other arithmetic, substep(): basis_one[:, :, None, None, :] * basis_two[:, None, :, None, :]  26 us
    reshape x4, local copies, waits for them, and re-layouts, neighbour_faces(): padded = padded.reshape(3, 4, 4, 4, sec_cells + 2, air_cells + 2)  18.9 us
    dot_general x4, matrix products, local_update(): applied = jnp.einsum('mn,cnse->cmse', operator, field, precision=exact_mode)  18.7 us
  transfers between devices with their start and end apart: 20, of which 8 were waited for; matrix products, arithmetic and copies ran while one was open for 10% of the time, Pallas kernels for 0%

commit v1 on v0

v1 whole, which is shorter than its diff:
```python
import functools
import jax, jax.numpy as jnp, numpy as np
from jax import lax
from jax.experimental import pallas as pl
from jax.experimental.pallas import tpu as pltpu

F32, BF16 = jnp.float32, jnp.bfloat16
BINS, GROUPS, SUB, SUBSTEPS = 192, 24, 8, 16
NT = (((1,), (1,)), ((), ()))
TN = (((0,), (0,)), ((), ()))

def dot(a, b, dims=(((1,), (0,)), ((), ()))):
    return lax.dot_general(a, b, dims, preferred_element_type=F32)

def split(x):
    hi = x.astype(BF16)
    return hi, (x - hi.astype(F32)).astype(BF16)

def basis(x):
    s = x * x
    outer = s * (9 / 16) - (1 / 16)
    inner = s * (27 / 16) - (27 / 16)
    return [outer - outer * x, inner * (x - 1 / 3), -(inner * (x + 1 / 3)), outer + outer * x]

def pairs(tiles):
    return [jnp.concatenate(tiles[i:i + 2], axis=0) for i in range(0, len(tiles), 2)]

def split_tiles(tiles):
    both = [split(p) for p in pairs(tiles)]
    return jnp.concatenate([b[0] for b in both], axis=0), jnp.concatenate([b[1] for b in both], axis=0)

def ioeq(shape, f):
    r = lax.broadcasted_iota(jnp.int32, shape, 0)
    c = lax.broadcasted_iota(jnp.int32, shape, 1)
    return jnp.where(f(r, c), 1.0, 0.0)

def drag_kernel(unroll, elem_col, elem_row, fill, fluid, mass, pos, vel, relax, coupled, pout, nodal, state, acc, dep):
    hi = jnp.zeros((BINS, BINS), F32)
    lo = jnp.zeros((BINS, BINS), F32)
    cols = lax.broadcasted_iota(jnp.int32, (BINS, 256), 1)
    for r in range(8):
        fh, fl = split(fluid[:, r, :])
        oh = jnp.where(elem_col[...] == cols + r * 256, 1.0, 0.0).astype(BF16)
        hi += dot(oh, fh, NT)
        lo += dot(oh, fl, NT)
    hi, lo = hi.astype(BF16), lo.astype(BF16)
    diag = ioeq((BINS, 128), lambda r, c: r % 8 == c % 8)
    for cp in range(6):
        for k, piece in enumerate((hi, lo)):
            both = []
            for ca in (2 * cp, 2 * cp + 1):
                rep = ioeq((BINS, 128), lambda r, c: r == ca * 16 + c // 8).astype(BF16)
                both.append((dot(piece, rep) * diag).reshape(GROUPS, 8, 128))
            both = jnp.concatenate(both, axis=1).astype(BF16)
            if k == 0:
                nodal[:, cp * 16:cp * 16 + 16, 0:128] = both
                nodal[:, cp * 16:cp * 16 + 16, 128:256] = both
            else:
                nodal[:, cp * 16:cp * 16 + 16, 256:384] = both
    occ = jnp.where(lax.broadcasted_iota(jnp.int32, (BINS, 128), 1) < fill[...], 1.0, 0.0)
    state[0:3] = pos[...]
    state[3:6] = vel[...]
    state[6] = relax[...] * occ
    state[7] = occ
    acc[...] = jnp.zeros_like(acc)

    def first(g):
        rows = pl.ds(pl.multiple_of(g * 8, 8), 8)
        x = [state[i, rows, :] for i in range(3)]
        l0, l1, l2 = (basis(t) for t in x)
        lh, ll = split_tiles([b * c for b in l1 for c in l2])
        return g, rows, x, l0, lh, ll, dot(nodal[g], jnp.concatenate([lh, ll, lh], axis=0))

    def second(args):
        g, rows, x, l0, lh, ll, both = args
        v = [state[3 + i, rows, :] for i in range(3)]
        ro, oc = state[6, rows, :], state[7, rows, :]
        stride = oc * 0.05
        forces = []
        for c in range(3):
            t = [l0[a] * both[(4 * c + a) * 8:(4 * c + a) * 8 + 8] for a in range(4)]
            u = (t[0] + t[1]) + (t[2] + t[3])
            dv = ro * (u - v[c])
            nv = v[c] + dv
            state[3 + c, rows, :] = nv
            state[c, rows, :] = jnp.clip(x[c] + stride * nv, -1.0, 1.0)
            forces += [dv * l0[a] for a in range(4)]
        fh, fl = split_tiles(forces)
        wa = jnp.concatenate([p.astype(BF16) for p in pairs([oc * (l * l) for l in l0])], axis=0)
        lt = lh.T
        drag = dot(jnp.concatenate([fh, fl, fh], axis=1), jnp.concatenate([lt, lt, ll.T], axis=0))
        return g, drag, dot(wa, lt * lt)

    def third(args):
        g, drag, weight = args
        acc[g, 0:96] += drag
        acc[g, 96:128] += weight

    def substep(t, _):
        def block(k, _):
            mid = [first(k * unroll + j) for j in range(unroll)]
            end = [second(m) for m in mid]
            for e in end: third(e)
            return 0
        lax.fori_loop(0, GROUPS // unroll, block, 0)
        return 0
    lax.fori_loop(0, SUBSTEPS, substep, 0)
    pout[...] = state[0:6]
    sums = jnp.zeros((BINS, 256), F32)
    for ca in range(16):
        a = acc[:, ca * 8:ca * 8 + 8, :].reshape(BINS, 128) * diag
        ah, al = split(a)
        rep = ioeq((256, 128), lambda r, c: r == ca * 16 + c // 8).astype(BF16)
        sums += dot(ah, rep, NT) + dot(al, rep, NT)
    sh, sl = split(sums.T)
    stacked = jnp.concatenate([sh, sl], axis=1)
    for r in range(8):
        oh = jnp.where(elem_col[...] == cols + r * 256, 1.0, 0.0).astype(BF16)
        dep[:, r, :] = dot(stacked, jnp.concatenate([oh, oh], axis=0))
    inv = 1.0 / (mass[...][None] + dep[192:256])
    for c in range(3):
        s = slice(c * 64, c * 64 + 64)
        coupled[s] = fluid[s] - dep[s] * inv

def drag(fluid, mass, pos, vel, relax, elem, fill, unroll=2):
    return pl.pallas_call(
        functools.partial(drag_kernel, unroll),
        out_shape=(jax.ShapeDtypeStruct((192, 8, 256), F32), jax.ShapeDtypeStruct((6, BINS, 128), F32)),
        scratch_shapes=[pltpu.VMEM((GROUPS, 96, 384), BF16), pltpu.VMEM((8, BINS, 128), F32),
                        pltpu.VMEM((GROUPS, 128, 128), F32), pltpu.VMEM((256, 8, 256), F32)],
        compiler_params=pltpu.CompilerParams(vmem_limit_bytes=56 * 2**20),
    )(elem.reshape(BINS, 1), elem.reshape(1, BINS), fill.reshape(BINS, 1), fluid, mass, pos, vel, relax)


PASSES = 4
MESH = pl.DeviceIdType.MESH


def curvature(line):
    low = line[0] - 2.0 * line[1] + line[2]
    high = line[1] - 2.0 * line[2] + line[3]
    step = low - high
    return [low + step, low, high, high - step]


CURVE = ((-2, 3, -1), (-1, 1, 0), (0, -1, 1), (1, -3, 2))
SLOPE = ((11, -7, 2), (2, 5, -1), (-1, 5, 2), (2, -7, 11))


def section_phase(src, dst, visc, sub):
    up = jnp.where(sub == 7, 0.0, 0.25)
    down = jnp.where(sub == 0, 0.0, 0.25)

    def body(i, _):
        base = pl.multiple_of(i * 16, 16)
        t = [[src[base + 4 * b + c] for c in range(4)] for b in range(4)]
        across = [curvature([t[b][c] for b in range(4)]) for c in range(4)]
        for b in range(4):
            along = curvature(t[b])
            for c in range(4):
                new = t[b][c] + visc * (along[c] + across[c][b])
                if b == 3:
                    new = new - 0.25 * t[3][c] + up * pltpu.roll(t[0][c], 7, 0)
                if b == 0:
                    new = new - 0.25 * t[0][c] + down * pltpu.roll(t[3][c], 1, 0)
                dst[base + 4 * b + c] = new
        return 0

    lax.fori_loop(0, 12, body, 0)


def airway_phase(src, dst, mix, lane):
    fore = jnp.where(lane == 255, 0.0, 0.25)
    back = jnp.where(lane == 0, 0.0, 0.25)

    def body(i, _):
        base = (i // 4) * 64 + (i % 4) * 4
        for c in range(4):
            at = [base + 16 * a + c for a in range(4)]
            q = [src[n] for n in at]
            d = [q[k + 1] - q[k] for k in range(3)]
            for a in range(4):
                new = dst[at[a]] + mix[3 * a] * d[0] + mix[3 * a + 1] * d[1] + mix[3 * a + 2] * d[2]
                if a == 3:
                    new = new - 0.25 * q[3] + fore * pltpu.roll(q[0], 255, 1)
                if a == 0:
                    new = new - 0.25 * q[0] + back * pltpu.roll(q[3], 1, 1)
                dst[at[a]] = new
        return 0

    lax.fori_loop(0, 12, body, 0)


def air_nodes(a):
    return [comp * 64 + a * 16 + k for comp in range(3) for k in range(16)]


def sec_nodes(b):
    return [comp * 64 + a * 16 + b * 4 + c for comp in range(3) for a in range(4) for c in range(4)]


def fluid_kernel(field, viscosity, speed, out, ping, pong, mix, s_sec, s_air, r_sec, r_air, send_sem, recv_sem):
    me_a, me_s = lax.axis_index("airway"), lax.axis_index("section")
    n_a, n_s = lax.axis_size("airway"), lax.axis_size("section")
    peers = [(me_a, lax.rem(me_s + 1, n_s)), (me_a, lax.rem(me_s + n_s - 1, n_s)),
             (lax.rem(me_a + 1, n_a), me_s), (lax.rem(me_a + n_a - 1, n_a), me_s)]
    barrier = pltpu.get_barrier_semaphore()
    for p in peers:
        pl.semaphore_signal(barrier, inc=1, device_id=p, device_id_type=MESH)
    visc = viscosity[...] * 2.25
    quarter = speed[...] * 0.25
    for a in range(4):
        for k in range(3):
            mix[3 * a + k] = CURVE[a][k] * visc - SLOPE[a][k] * quarter
    sub = lax.broadcasted_iota(jnp.int32, (8, 256), 0)
    lane = lax.broadcasted_iota(jnp.int32, (8, 256), 1)
    lane1 = lax.broadcasted_iota(jnp.int32, (8, 128), 1)
    some = lambda cond: jnp.where(cond, 0.25, 0.0).astype(F32)
    next_s, prev_s = some(me_s < n_s - 1), some(me_s > 0)
    next_a, prev_a = some(me_a < n_a - 1), some(me_a > 0)
    pl.semaphore_wait(barrier, 4)
    bufs = [field, ping, pong, ping, out]
    for p in range(PASSES):
        src, dst = bufs[p], bufs[p + 1]
        for slot, row, b in ((0, 7, 3), (1, 0, 0)):
            for j, n in enumerate(sec_nodes(b)):
                s_sec[p, slot, j:j + 1, :] = src[n, row:row + 1, :]
        for slot, base, a in ((0, 128, 3), (1, 0, 0)):
            packed = jnp.zeros((8, 128), F32)
            col = 127 if slot == 0 else 0
            for j, n in enumerate(air_nodes(a)):
                moved = pltpu.roll(src[n, :, base:base + 128], (j - col) % 128, 1)
                packed = jnp.where(lane1 == j, moved, packed)
            s_air[p, slot] = packed
        copies = []
        for k in range(4):
            s, r = (s_sec, r_sec) if k < 2 else (s_air, r_air)
            copies.append(pltpu.make_async_remote_copy(
                src_ref=s.at[p, k % 2], dst_ref=r.at[p, k % 2], send_sem=send_sem.at[p, k], recv_sem=recv_sem.at[p, k],
                device_id=peers[k], device_id_type=MESH))
            copies[-1].start()
        section_phase(src, dst, visc, sub)
        airway_phase(src, dst, mix, lane)
        for c in copies:
            c.wait()
        for slot, row, b, scale in ((0, 0, 0, prev_s), (1, 7, 3, next_s)):
            for j, n in enumerate(sec_nodes(b)):
                dst[n, row:row + 1, :] += scale * r_sec[p, slot, j:j + 1, :]
        for slot, base, a, scale in ((0, 0, 0, prev_a), (1, 128, 3, next_a)):
            col = 0 if slot == 0 else 127
            packed = r_air[p, slot] * scale
            for j, n in enumerate(air_nodes(a)):
                moved = pltpu.roll(packed, (col - j) % 128, 1)
                dst[n, :, base:base + 128] += jnp.where(lane1 == col, moved, 0.0)


def advance(field, viscosity, speed):
    vm = pl.BlockSpec(memory_space=pltpu.VMEM)
    return pl.pallas_call(
        fluid_kernel,
        out_shape=jax.ShapeDtypeStruct((192, 8, 256), F32),
        in_specs=[vm] * 3,
        out_specs=vm,
        scratch_shapes=[pltpu.VMEM((192, 8, 256), F32), pltpu.VMEM((192, 8, 256), F32), pltpu.VMEM((12, 8, 256), F32),
                        pltpu.VMEM((PASSES, 2, 48, 256), F32), pltpu.VMEM((PASSES, 2, 8, 128), F32),
                        pltpu.VMEM((PASSES, 2, 48, 256), F32), pltpu.VMEM((PASSES, 2, 8, 128), F32),
                        pltpu.SemaphoreType.DMA((PASSES, 4)), pltpu.SemaphoreType.DMA((PASSES, 4))],
        compiler_params=pltpu.CompilerParams(collective_id=0, has_side_effects=True, vmem_limit_bytes=56 * 2**20),
    )(field, viscosity, speed)

def local(fluid_velocity, viscosity, axial_speed, fluid_mass, positions, velocities, relax_rates, bin_element, bin_fill):
    field = fluid_velocity.reshape(192, 8, 256)
    coupled, moved = drag(field, fluid_mass, positions.transpose(1, 0, 2), velocities.transpose(1, 0, 2), relax_rates,
                          bin_element, bin_fill, 8)
    return advance(coupled, viscosity, axial_speed).reshape(fluid_velocity.shape), moved.transpose(1, 0, 2)


def solution(mesh):
    from jax.sharding import PartitionSpec as P
    bins = ("airway", "section")
    cells = P("section", "airway")
    return jax.shard_map(
        local,
        mesh=mesh,
        in_specs=(P(None, None, *cells), cells, cells, cells, P(bins, None, None), P(bins, None, None), P(bins, None),
                  P(bins), P(bins)),
        out_specs=(P(None, None, *cells), P(bins, None, None)),
        check_vma=False,
    )
```

time: 677 us -> 75.3 us (0.11); the launches traced: 666 us -> 75.1 us
  matrix products: 292 us -> 0 us
  other arithmetic: 100 us -> 0 us
  local copies, waits for them, and re-layouts: 93.7 us -> 5.53 us
  Pallas kernels: 0 us -> 68.9 us
  blocking collectives: 68.1 us -> 0 us
  starting transfers between devices: 62.5 us -> 0 us
  waiting for transfers between devices: 42.3 us -> 0 us
    dot_general x53 -> x0, matrix products: 292 us -> none  [the longest x16 107 us: substep(): jnp.einsum('bnp,bcp->bcn', weights, change, precision=exact_mode)]
    pallas_call x0 -> x2, Pallas kernels: none -> 68.9 us  [the longest x1 39.4 us: drag(): pl.pallas_call(functools.partial(drag_kernel, unroll), out_shape=(jax.Sha...]
    unnamed x1 -> x0, blocking collectives: 68.1 us -> none
    ppermute x16 -> x0, starting transfers between devices: 38.2 us -> none  [the longest x8 27.9 us: with_halo(): lax.ppermute(tail, axis, [(i, (i + 1) % count) for i in range(ends)])]
    mul x55 -> x0, other arithmetic: 30.4 us -> none  [the longest x32 26 us: substep(): basis_one[:, :, None, None, :] * basis_two[:, None, :, None, :]]
    all_to_all x4 -> x0, waiting for transfers between devices: 27 us -> none  [the longest x1 12.5 us: send_bins(): lax.all_to_all(out_records, ('airway', 'section'), split_axis=0, concat_a...]
    all_to_all x4 -> x0, starting transfers between devices: 24.2 us -> none  [the longest x1 9.87 us: return_bins(): lax.all_to_all(back_state, ('airway', 'section'), split_axis=0, concat_ax...]
    concatenate x16 -> x0, other arithmetic: 19.9 us -> none  [the longest x8 17.4 us: with_halo(): jnp.concatenate([lax.ppermute(tail, axis, [(i, (i + 1) % count) for i in...]
  transfers between devices with their start and end apart: 20 -> 0, of which waited for: 8 -> 0; matrix products, arithmetic and copies ran while one was open for 10% -> 0% of each run, Pallas kernels for 0% -> 0%
where the time goes in v1:
time: 75.3 us; the launch traced here: 75.1 us
  Pallas kernels  68.9 us (92%)
  local copies, waits for them, and re-layouts  5.53 us (7%)
    pallas_call x1, Pallas kernels, drag(): pl.pallas_call(functools.partial(drag_kernel, unroll), out_shape=(jax.Sha...  39.4 us
    pallas_call x1, Pallas kernels, advance(): pl.pallas_call(fluid_kernel, out_shape=jax.ShapeDtypeStruct((192, 8, 256)...  29.4 us
    unnamed x1, local copies, waits for them, and re-layouts  2.65 us

profile of v1, /device:TPU:0, one launch (start us, length us, event | category | flops | bytes accessed | tf_op | source)
XLA Modules:
  0.0 75.1 jit_solution(18313093194336512609)
XLA Ops:
  0.6 1.4 %copy.12.fill = s32[192,1]{1,0:T(8,128)} copy(s32[192,1]{0,1:T(1,128)} %bitcast.14) | data formatting | bytes 1536 | tf_op jit(solution)/shard_map/reshape | solution.py:132
  2.1 1.4 %copy.11.elem_col = s32[192,1]{1,0:T(8,128)} copy(s32[192,1]{0,1:T(1,128)} %bitcast.12) | data formatting | bytes 1536 | tf_op jit(solution)/shard_map/reshape | solution.py:132
  3.5 39.4 %shard_map.104 = (f32[192,8,256]{2,1,0:T(8,128)}, f32[6,192,128]{2,1,0:T(8,128)}) custom-call(s32[192,1]{1,0:T(8,128)} %copy.11.elem_col, s32[1,192]{1,0:T(1,128)} %bitcast.13, s32[192,1]{1,0:T(8,128)} %copy.12.fill, f32[192,8,256]{2,1,0:T(8,128)} %bitcast.9, f32[8,256]{1,0:T(8,128)} %mass.1, f32[3,192,128]{2,1,0:T(8,128)} %bitcast.10, ...), custom_call_target="tpu_custom_call" | custom-call | tf_op jit(solution)/shard_map/pallas_call | solution.py:126
  42.9 29.4 %shard_map.105 = f32[192,8,256]{2,1,0:T(8,128)} custom-call(f32[192,8,256]{2,1,0:T(8,128)} %get-tuple-element.4.field, f32[8,256]{1,0:T(8,128)} %viscosity.1, f32[8,256]{1,0:T(8,128)} %speed.1), custom_call_target="tpu_custom_call" | custom-call | tf_op jit(solution)/shard_map/pallas_call | solution.py:259
  72.4 2.7 %copy.14 = f32[3,64,8,256]{3,2,1,0:T(8,128)} copy(f32[3,64,8,256]{3,2,1,0:T(8,128)} %bitcast.8) | data formatting | bytes 3145728

commit v2 on v1

--- a/solution.py
+++ b/solution.py
@@ -3,133 +3,158 @@
 from jax import lax
 from jax.experimental import pallas as pl
 from jax.experimental.pallas import tpu as pltpu
+from jax.sharding import PartitionSpec as P
 
 F32, BF16 = jnp.float32, jnp.bfloat16
-BINS, GROUPS, SUB, SUBSTEPS = 192, 24, 8, 16
-NT = (((1,), (1,)), ((), ()))
-TN = (((0,), (0,)), ((), ()))
-
-def dot(a, b, dims=(((1,), (0,)), ((), ()))):
-    return lax.dot_general(a, b, dims, preferred_element_type=F32)
+BINS, GROUPS, SUBSTEPS = 192, 24, 16
+cat = jnp.concatenate
+
+
+def dot(a, b):
+    return jnp.dot(a, b, preferred_element_type=F32)
+
 
 def split(x):
     hi = x.astype(BF16)
     return hi, (x - hi.astype(F32)).astype(BF16)
+
 
 def basis(x):
     s = x * x
     outer = s * (9 / 16) - (1 / 16)
     inner = s * (27 / 16) - (27 / 16)
-    return [outer - outer * x, inner * (x - 1 / 3), -(inner * (x + 1 / 3)), outer + outer * x]
+    ends, mids = outer * x, inner * x
+    third = inner * (1 / 3)
+    return [outer - ends, mids - third, -(mids + third), outer + ends]
+
 
 def pairs(tiles):
-    return [jnp.concatenate(tiles[i:i + 2], axis=0) for i in range(0, len(tiles), 2)]
+    return [cat(tiles[i:i + 2], axis=0) for i in range(0, len(tiles), 2)]
+
 
 def split_tiles(tiles):
     both = [split(p) for p in pairs(tiles)]
-    return jnp.concatenate([b[0] for b in both], axis=0), jnp.concatenate([b[1] for b in both], axis=0)
-
-def ioeq(shape, f):
+    return cat([b[0] for b in both], axis=0), cat([b[1] for b in both], axis=0)
+
+
+def ones_where(shape, same):
     r = lax.broadcasted_iota(jnp.int32, shape, 0)
     c = lax.broadcasted_iota(jnp.int32, shape, 1)
-    return jnp.where(f(r, c), 1.0, 0.0)
-
-def drag_kernel(unroll, elem_col, elem_row, fill, fluid, mass, pos, vel, relax, coupled, pout, nodal, state, acc, dep):
-    hi = jnp.zeros((BINS, BINS), F32)
-    lo = jnp.zeros((BINS, BINS), F32)
-    cols = lax.broadcasted_iota(jnp.int32, (BINS, 256), 1)
+    return jnp.where(same(r, c), 1.0, 0.0)
+
+
+def drag_kernel(unroll, elem, fill, fluid, mass, pos, vel, relax, coupled, pout,
+                nodal, state, acc, s_basis, s_nodal, s_first):
+    diag = ones_where((BINS, 128), lambda r, c: r % 8 == c % 8)
+    column = jnp.broadcast_to(elem[...].astype(F32), (128, BINS)).T
+    column = cat([column, column], axis=1)
+    got = jnp.zeros((2 * BINS, BINS), F32)
+    cells = lax.broadcasted_iota(jnp.int32, (256, BINS), 0)
     for r in range(8):
-        fh, fl = split(fluid[:, r, :])
-        oh = jnp.where(elem_col[...] == cols + r * 256, 1.0, 0.0).astype(BF16)
-        hi += dot(oh, fh, NT)
-        lo += dot(oh, fl, NT)
-    hi, lo = hi.astype(BF16), lo.astype(BF16)
-    diag = ioeq((BINS, 128), lambda r, c: r % 8 == c % 8)
+        hot = jnp.where(cells + r * 256 == elem[...], 1.0, 0.0).astype(BF16)
+        got += dot(cat(split(fluid[:, r, :]), axis=0), hot)
+    got = cat([got[:BINS].T, got[BINS:].T], axis=0).astype(BF16)
+    mask = diag.astype(BF16)
     for cp in range(6):
-        for k, piece in enumerate((hi, lo)):
-            both = []
-            for ca in (2 * cp, 2 * cp + 1):
-                rep = ioeq((BINS, 128), lambda r, c: r == ca * 16 + c // 8).astype(BF16)
-                both.append((dot(piece, rep) * diag).reshape(GROUPS, 8, 128))
-            both = jnp.concatenate(both, axis=1).astype(BF16)
-            if k == 0:
-                nodal[:, cp * 16:cp * 16 + 16, 0:128] = both
-                nodal[:, cp * 16:cp * 16 + 16, 128:256] = both
-            else:
-                nodal[:, cp * 16:cp * 16 + 16, 256:384] = both
-    occ = jnp.where(lax.broadcasted_iota(jnp.int32, (BINS, 128), 1) < fill[...], 1.0, 0.0)
+        rep = ones_where((BINS, 256), lambda r, c: r == (2 * cp + c // 128) * 16 + (c % 128) // 8).astype(BF16)
+        wide = dot(got, rep)
+        tile = []
+        for k in range(2):
+            part = wide[k * BINS:(k + 1) * BINS]
+            two = [(part[:, 128 * j:128 * j + 128] * diag).reshape(GROUPS, 8, 128) for j in range(2)]
+            tile.append(cat(two, axis=1).astype(BF16))
+        nodal[:, cp * 16:cp * 16 + 16, 0:128] = tile[0]
+        nodal[:, cp * 16:cp * 16 + 16, 128:256] = tile[0]
+        nodal[:, cp * 16:cp * 16 + 16, 256:384] = tile[1]
+    slots = lax.broadcasted_iota(jnp.int32, (128, BINS), 0)
+    occ = jnp.where(slots < fill[...], 1.0, 0.0).T
     state[0:3] = pos[...]
     state[3:6] = vel[...]
     state[6] = relax[...] * occ
     state[7] = occ
     acc[...] = jnp.zeros_like(acc)
 
-    def first(g):
+    def first(g, slot):
+        rows = pl.ds(pl.multiple_of(g * 8, 8), 8)
+        l0, l1, l2 = (basis(state[i, rows, :]) for i in range(3))
+        lh, ll = split_tiles([b * c for b in l1 for c in l2])
+        for a in range(4):
+            s_first[slot, a] = l0[a]
+        s_basis[slot, 0:128] = lh
+        s_basis[slot, 128:256] = ll
+        s_nodal[slot] = dot(nodal[g], cat([lh, ll, lh], axis=0))
+
+    def second(g, slot):
         rows = pl.ds(pl.multiple_of(g * 8, 8), 8)
         x = [state[i, rows, :] for i in range(3)]
-        l0, l1, l2 = (basis(t) for t in x)
-        lh, ll = split_tiles([b * c for b in l1 for c in l2])
-        return g, rows, x, l0, lh, ll, dot(nodal[g], jnp.concatenate([lh, ll, lh], axis=0))
-
-    def second(args):
-        g, rows, x, l0, lh, ll, both = args
         v = [state[3 + i, rows, :] for i in range(3)]
         ro, oc = state[6, rows, :], state[7, rows, :]
+        l0 = [s_first[slot, a] for a in range(4)]
         stride = oc * 0.05
         forces = []
         for c in range(3):
-            t = [l0[a] * both[(4 * c + a) * 8:(4 * c + a) * 8 + 8] for a in range(4)]
-            u = (t[0] + t[1]) + (t[2] + t[3])
-            dv = ro * (u - v[c])
+            t = [l0[a] * s_nodal[slot, (4 * c + a) * 8:(4 * c + a) * 8 + 8] for a in range(4)]
+            dv = ro * (((t[0] + t[1]) + (t[2] + t[3])) - v[c])
             nv = v[c] + dv
             state[3 + c, rows, :] = nv
             state[c, rows, :] = jnp.clip(x[c] + stride * nv, -1.0, 1.0)
             forces += [dv * l0[a] for a in range(4)]
         fh, fl = split_tiles(forces)
-        wa = jnp.concatenate([p.astype(BF16) for p in pairs([oc * (l * l) for l in l0])], axis=0)
-        lt = lh.T
-        drag = dot(jnp.concatenate([fh, fl, fh], axis=1), jnp.concatenate([lt, lt, ll.T], axis=0))
-        return g, drag, dot(wa, lt * lt)
-
-    def third(args):
-        g, drag, weight = args
-        acc[g, 0:96] += drag
-        acc[g, 96:128] += weight
-
-    def substep(t, _):
-        def block(k, _):
-            mid = [first(k * unroll + j) for j in range(unroll)]
-            end = [second(m) for m in mid]
-            for e in end: third(e)
-            return 0
-        lax.fori_loop(0, GROUPS // unroll, block, 0)
+        wa = cat([p.astype(BF16) for p in pairs([oc * (l * l) for l in l0])], axis=0)
+        lt, llt = s_basis[slot, 0:128].T, s_basis[slot, 128:256].T
+        acc[g, 0:96] += dot(cat([fh, fl, fh], axis=1), cat([lt, lt, llt], axis=0))
+        acc[g, 96:128] += dot(wa, lt * lt)
+
+    blocks = GROUPS // unroll
+
+    def run(stage, i, side):
+        for j in range(unroll):
+            stage(lax.rem(i, blocks) * unroll + j, side * unroll + j)
+
+    run(first, 0, 0)
+
+    def body(k, _):
+        i = 2 * k
+        run(first, i + 1, 1)
+        run(second, i, 0)
+        run(first, i + 2, 0)
+        run(second, i + 1, 1)
         return 0
-    lax.fori_loop(0, SUBSTEPS, substep, 0)
+
+    n = SUBSTEPS * blocks
+    lax.fori_loop(0, n // 2 - 1, body, 0)
+    run(first, n - 1, 1)
+    run(second, n - 2, 0)
+    run(second, n - 1, 1)
     pout[...] = state[0:6]
-    sums = jnp.zeros((BINS, 256), F32)
-    for ca in range(16):
-        a = acc[:, ca * 8:ca * 8 + 8, :].reshape(BINS, 128) * diag
-        ah, al = split(a)
-        rep = ioeq((256, 128), lambda r, c: r == ca * 16 + c // 8).astype(BF16)
-        sums += dot(ah, rep, NT) + dot(al, rep, NT)
-    sh, sl = split(sums.T)
-    stacked = jnp.concatenate([sh, sl], axis=1)
+    sums = jnp.zeros((2 * BINS, 256), F32)
+    for cp in range(8):
+        two = cat([acc[:, (2 * cp + j) * 8:(2 * cp + j) * 8 + 8, :].reshape(BINS, 128) * diag for j in range(2)], axis=1)
+        rep = ones_where((256, 256), lambda r, c: c == (2 * cp + r // 128) * 16 + (r % 128) // 8).astype(BF16)
+        sums += dot(cat(split(two), axis=0), rep)
+    sums = cat(split((sums[:BINS] + sums[BINS:]).T), axis=1)
+    lanes = lax.broadcasted_iota(jnp.int32, (BINS, 256), 1).astype(F32)
     for r in range(8):
-        oh = jnp.where(elem_col[...] == cols + r * 256, 1.0, 0.0).astype(BF16)
-        dep[:, r, :] = dot(stacked, jnp.concatenate([oh, oh], axis=0))
-    inv = 1.0 / (mass[...][None] + dep[192:256])
-    for c in range(3):
-        s = slice(c * 64, c * 64 + 64)
-        coupled[s] = fluid[s] - dep[s] * inv
-
-def drag(fluid, mass, pos, vel, relax, elem, fill, unroll=2):
+        hot = jnp.where(column == lanes + float(r * 256), 1.0, 0.0).astype(BF16)
+        dep = dot(sums, cat([hot, hot], axis=0))
+        inv = 1.0 / (mass[r:r + 1, :] + dep[192:256])
+        for c in range(3):
+            s = slice(c * 64, c * 64 + 64)
+            coupled[s, r, :] = fluid[s, r, :] - dep[s] * inv
+
+
+def drag(fluid, mass, pos, vel, relax, elem, fill, unroll=4):
+    vm = pl.BlockSpec(memory_space=pltpu.VMEM)
     return pl.pallas_call(
         functools.partial(drag_kernel, unroll),
         out_shape=(jax.ShapeDtypeStruct((192, 8, 256), F32), jax.ShapeDtypeStruct((6, BINS, 128), F32)),
+        in_specs=[vm] * 7,
+        out_specs=(vm, vm),
         scratch_shapes=[pltpu.VMEM((GROUPS, 96, 384), BF16), pltpu.VMEM((8, BINS, 128), F32),
-                        pltpu.VMEM((GROUPS, 128, 128), F32), pltpu.VMEM((256, 8, 256), F32)],
+                        pltpu.VMEM((GROUPS, 128, 128), F32), pltpu.VMEM((2 * unroll, 256, 128), BF16),
+                        pltpu.VMEM((2 * unroll, 96, 128), F32), pltpu.VMEM((2 * unroll, 4, 8, 128), F32)],
         compiler_params=pltpu.CompilerParams(vmem_limit_bytes=56 * 2**20),
-    )(elem.reshape(BINS, 1), elem.reshape(1, BINS), fill.reshape(BINS, 1), fluid, mass, pos, vel, relax)
+    )(elem.reshape(1, BINS), fill.reshape(1, BINS), fluid, mass, pos, vel, relax)
 
 
 PASSES = 4
@@ -271,12 +296,11 @@
 def local(fluid_velocity, viscosity, axial_speed, fluid_mass, positions, velocities, relax_rates, bin_element, bin_fill):
     field = fluid_velocity.reshape(192, 8, 256)
     coupled, moved = drag(field, fluid_mass, positions.transpose(1, 0, 2), velocities.transpose(1, 0, 2), relax_rates,
-                          bin_element, bin_fill, 8)
+                          bin_element, bin_fill, 12)
     return advance(coupled, viscosity, axial_speed).reshape(fluid_velocity.shape), moved.transpose(1, 0, 2)
 
 
 def solution(mesh):
-    from jax.sharding import PartitionSpec as P
     bins = ("airway", "section")
     cells = P("section", "airway")
     return jax.shard_map(

time: 75.3 us -> 67.8 us (0.900)
  Pallas kernels: 68.9 us -> 64.3 us
  local copies, waits for them, and re-layouts: 5.53 us -> 2.65 us
    pallas_call x1, Pallas kernels: 39.4 us -> 34.8 us  [drag(): pl.pallas_call(functools.partial(drag_kernel, unroll), out_shape=(jax.Sha...]
    reshape x2 -> x0, local copies, waits for them, and re-layouts: 2.88 us -> none  [the longest x1 1.44 us: drag(): fill.reshape(BINS, 1)]
where the time goes in v2:
time: 67.8 us; the launch traced here: 67.6 us
  Pallas kernels  64.3 us (95%)
  local copies, waits for them, and re-layouts  2.65 us (4%)
    pallas_call x1, Pallas kernels, drag(): pl.pallas_call(functools.partial(drag_kernel, unroll), out_shape=(jax.Sha...  34.8 us
    pallas_call x1, Pallas kernels, advance(): pl.pallas_call(fluid_kernel, out_shape=jax.ShapeDtypeStruct((192, 8, 256)...  29.4 us
    unnamed x1, local copies, waits for them, and re-layouts  2.65 us

profile of v2, /device:TPU:0, one launch (start us, length us, event | category | flops | bytes accessed | tf_op | source)
XLA Modules:
  0.0 67.6 jit_solution(13390213472217139545)
XLA Ops:
  0.6 34.8 %shard_map.104 = (f32[192,8,256]{2,1,0:T(8,128)}, f32[6,192,128]{2,1,0:T(8,128)}) custom-call(s32[1,192]{1,0:T(1,128)} %bitcast.11, s32[1,192]{1,0:T(1,128)} %bitcast.12, f32[192,8,256]{2,1,0:T(8,128)} %bitcast.8, f32[8,256]{1,0:T(8,128)} %mass.1, f32[3,192,128]{2,1,0:T(8,128)} %bitcast.9, f32[3,192,128]{2,1,0:T(8,128)} %bitcast.10, f32[192,128]{1,0:T(8,128)} %relax.1), custom_call_target="tpu_custom_call" | custom-call | tf_op jit(solution)/shard_map/pallas_call | solution.py:148
  35.5 29.4 %shard_map.105 = f32[192,8,256]{2,1,0:T(8,128)} custom-call(f32[192,8,256]{2,1,0:T(8,128)} %get-tuple-element.4.field, f32[8,256]{1,0:T(8,128)} %viscosity.1, f32[8,256]{1,0:T(8,128)} %speed.1), custom_call_target="tpu_custom_call" | custom-call | tf_op jit(solution)/shard_map/pallas_call | solution.py:284
  64.9 2.7 %copy.12 = f32[3,64,8,256]{3,2,1,0:T(8,128)} copy(f32[3,64,8,256]{3,2,1,0:T(8,128)} %bitcast.7) | data formatting | bytes 3145728

commit v3 on v2

--- a/solution.py
+++ b/solution.py
@@ -52,11 +52,11 @@
     cells = lax.broadcasted_iota(jnp.int32, (256, BINS), 0)
     for r in range(8):
         hot = jnp.where(cells + r * 256 == elem[...], 1.0, 0.0).astype(BF16)
-        got += dot(cat(split(fluid[:, r, :]), axis=0), hot)
+        got += dot(cat(split(cat([fluid[pl.ds(8 * h + r, BINS, stride=16), :] for h in range(2)], axis=1)), axis=0), hot)
     got = cat([got[:BINS].T, got[BINS:].T], axis=0).astype(BF16)
     mask = diag.astype(BF16)
     for cp in range(6):
-        rep = ones_where((BINS, 256), lambda r, c: r == (2 * cp + c // 128) * 16 + (c % 128) // 8).astype(BF16)
+        rep = ones_where((BINS, 256), lambda r, c: r == cp * 32 + (c >> 3)).astype(BF16)
         wide = dot(got, rep)
         tile = []
         for k in range(2):
@@ -130,7 +130,7 @@
     sums = jnp.zeros((2 * BINS, 256), F32)
     for cp in range(8):
         two = cat([acc[:, (2 * cp + j) * 8:(2 * cp + j) * 8 + 8, :].reshape(BINS, 128) * diag for j in range(2)], axis=1)
-        rep = ones_where((256, 256), lambda r, c: c == (2 * cp + r // 128) * 16 + (r % 128) // 8).astype(BF16)
+        rep = ones_where((256, 256), lambda r, c: c == cp * 32 + (r >> 3)).astype(BF16)
         sums += dot(cat(split(two), axis=0), rep)
     sums = cat(split((sums[:BINS] + sums[BINS:]).T), axis=1)
     lanes = lax.broadcasted_iota(jnp.int32, (BINS, 256), 1).astype(F32)
@@ -139,22 +139,29 @@
         dep = dot(sums, cat([hot, hot], axis=0))
         inv = 1.0 / (mass[r:r + 1, :] + dep[192:256])
         for c in range(3):
-            s = slice(c * 64, c * 64 + 64)
-            coupled[s, r, :] = fluid[s, r, :] - dep[s] * inv
-
-
-def drag(fluid, mass, pos, vel, relax, elem, fill, unroll=4):
+            change = dep[c * 64:c * 64 + 64] * inv
+            for h in range(2):
+                s = pl.ds(c * 1024 + 8 * h + r, 64, stride=16)
+                coupled[s, :] = fluid[s, :] - change[:, 128 * h:128 * h + 128]
+
+
+def drag(*a, **k):
+    q, p = drag_(*a, **k)
+    return q.reshape(192, 2, 8, 128).transpose(0, 2, 1, 3).reshape(192, 8, 256), p
+
+
+def drag_(fluid, mass, pos, vel, relax, elem, fill, unroll=4):
     vm = pl.BlockSpec(memory_space=pltpu.VMEM)
     return pl.pallas_call(
         functools.partial(drag_kernel, unroll),
-        out_shape=(jax.ShapeDtypeStruct((192, 8, 256), F32), jax.ShapeDtypeStruct((6, BINS, 128), F32)),
+        out_shape=(jax.ShapeDtypeStruct((3072, 128), F32), jax.ShapeDtypeStruct((6, BINS, 128), F32)),
         in_specs=[vm] * 7,
         out_specs=(vm, vm),
         scratch_shapes=[pltpu.VMEM((GROUPS, 96, 384), BF16), pltpu.VMEM((8, BINS, 128), F32),
                         pltpu.VMEM((GROUPS, 128, 128), F32), pltpu.VMEM((2 * unroll, 256, 128), BF16),
                         pltpu.VMEM((2 * unroll, 96, 128), F32), pltpu.VMEM((2 * unroll, 4, 8, 128), F32)],
         compiler_params=pltpu.CompilerParams(vmem_limit_bytes=56 * 2**20),
-    )(elem.reshape(1, BINS), fill.reshape(1, BINS), fluid, mass, pos, vel, relax)
+    )(elem.reshape(1, BINS), fill.reshape(1, BINS), fluid.reshape(192, 8, 2, 128).transpose(0, 2, 1, 3).reshape(3072, 128), mass, pos, vel, relax)
 
 
 PASSES = 4
@@ -172,12 +179,12 @@
 SLOPE = ((11, -7, 2), (2, 5, -1), (-1, 5, 2), (2, -7, 11))
 
 
-def section_phase(src, dst, visc, sub):
+def section_phase(src, dst, visc, sub, comp):
     up = jnp.where(sub == 7, 0.0, 0.25)
     down = jnp.where(sub == 0, 0.0, 0.25)
 
     def body(i, _):
-        base = pl.multiple_of(i * 16, 16)
+        base = comp * 64 + i * 16
         t = [[src[base + 4 * b + c] for c in range(4)] for b in range(4)]
         across = [curvature([t[b][c] for b in range(4)]) for c in range(4)]
         for b in range(4):
@@ -191,15 +198,15 @@
                 dst[base + 4 * b + c] = new
         return 0
 
-    lax.fori_loop(0, 12, body, 0)
-
-
-def airway_phase(src, dst, mix, lane):
+    lax.fori_loop(0, 4, body, 0, unroll=2)
+
+
+def airway_phase(src, dst, mix, lane, comp):
     fore = jnp.where(lane == 255, 0.0, 0.25)
     back = jnp.where(lane == 0, 0.0, 0.25)
 
     def body(i, _):
-        base = (i // 4) * 64 + (i % 4) * 4
+        base = comp * 64 + i * 4
         for c in range(4):
             at = [base + 16 * a + c for a in range(4)]
             q = [src[n] for n in at]
@@ -213,15 +220,15 @@
                 dst[at[a]] = new
         return 0
 
-    lax.fori_loop(0, 12, body, 0)
-
-
-def air_nodes(a):
-    return [comp * 64 + a * 16 + k for comp in range(3) for k in range(16)]
-
-
-def sec_nodes(b):
-    return [comp * 64 + a * 16 + b * 4 + c for comp in range(3) for a in range(4) for c in range(4)]
+    lax.fori_loop(0, 4, body, 0, unroll=2)
+
+
+def air_nodes(a, comp):
+    return [comp * 64 + a * 16 + k for k in range(16)]
+
+
+def sec_nodes(b, comp):
+    return [comp * 64 + a * 16 + b * 4 + c for a in range(4) for c in range(4)]
 
 
 def fluid_kernel(field, viscosity, speed, out, ping, pong, mix, s_sec, s_air, r_sec, r_air, send_sem, recv_sem):
@@ -245,38 +252,53 @@
     next_a, prev_a = some(me_a < n_a - 1), some(me_a > 0)
     pl.semaphore_wait(barrier, 4)
     bufs = [field, ping, pong, ping, out]
-    for p in range(PASSES):
-        src, dst = bufs[p], bufs[p + 1]
+    flying = {}
+
+    def send(p, comp):
+        src = bufs[p]
         for slot, row, b in ((0, 7, 3), (1, 0, 0)):
-            for j, n in enumerate(sec_nodes(b)):
-                s_sec[p, slot, j:j + 1, :] = src[n, row:row + 1, :]
+            for j, n in enumerate(sec_nodes(b, comp)):
+                s_sec[p, comp, slot, j:j + 1, :] = src[n, row:row + 1, :]
+        copies = [start(p, comp, k, s_sec, r_sec) for k in (0, 1)]
         for slot, base, a in ((0, 128, 3), (1, 0, 0)):
             packed = jnp.zeros((8, 128), F32)
             col = 127 if slot == 0 else 0
-            for j, n in enumerate(air_nodes(a)):
+            for j, n in enumerate(air_nodes(a, comp)):
                 moved = pltpu.roll(src[n, :, base:base + 128], (j - col) % 128, 1)
                 packed = jnp.where(lane1 == j, moved, packed)
-            s_air[p, slot] = packed
-        copies = []
-        for k in range(4):
-            s, r = (s_sec, r_sec) if k < 2 else (s_air, r_air)
-            copies.append(pltpu.make_async_remote_copy(
-                src_ref=s.at[p, k % 2], dst_ref=r.at[p, k % 2], send_sem=send_sem.at[p, k], recv_sem=recv_sem.at[p, k],
-                device_id=peers[k], device_id_type=MESH))
-            copies[-1].start()
-        section_phase(src, dst, visc, sub)
-        airway_phase(src, dst, mix, lane)
-        for c in copies:
+            s_air[p, comp, slot] = packed
+        flying[p, comp] = copies + [start(p, comp, k, s_air, r_air) for k in (2, 3)]
+
+    def start(p, comp, k, s, r):
+        copy = pltpu.make_async_remote_copy(
+            src_ref=s.at[p, comp, k % 2], dst_ref=r.at[p, comp, k % 2], send_sem=send_sem.at[p, comp, k],
+            recv_sem=recv_sem.at[p, comp, k], device_id=peers[k], device_id_type=MESH)
+        copy.start()
+        return copy
+
+    def receive(p, comp):
+        dst = bufs[p + 1]
+        for c in flying[p, comp]:
             c.wait()
         for slot, row, b, scale in ((0, 0, 0, prev_s), (1, 7, 3, next_s)):
-            for j, n in enumerate(sec_nodes(b)):
-                dst[n, row:row + 1, :] += scale * r_sec[p, slot, j:j + 1, :]
+            for j, n in enumerate(sec_nodes(b, comp)):
+                dst[n, row:row + 1, :] += scale * r_sec[p, comp, slot, j:j + 1, :]
         for slot, base, a, scale in ((0, 0, 0, prev_a), (1, 128, 3, next_a)):
             col = 0 if slot == 0 else 127
-            packed = r_air[p, slot] * scale
-            for j, n in enumerate(air_nodes(a)):
+            packed = r_air[p, comp, slot] * scale
+            for j, n in enumerate(air_nodes(a, comp)):
                 moved = pltpu.roll(packed, (col - j) % 128, 1)
                 dst[n, :, base:base + 128] += jnp.where(lane1 == col, moved, 0.0)
+
+    for p in range(PASSES):
+        for comp in range(3):
+            if p:
+                receive(p - 1, comp)
+            send(p, comp)
+            section_phase(bufs[p], bufs[p + 1], visc, sub, comp)
+            airway_phase(bufs[p], bufs[p + 1], mix, lane, comp)
+    for comp in range(3):
+        receive(PASSES - 1, comp)
 
 
 def advance(field, viscosity, speed):
@@ -287,9 +309,9 @@
         in_specs=[vm] * 3,
         out_specs=vm,
         scratch_shapes=[pltpu.VMEM((192, 8, 256), F32), pltpu.VMEM((192, 8, 256), F32), pltpu.VMEM((12, 8, 256), F32),
-                        pltpu.VMEM((PASSES, 2, 48, 256), F32), pltpu.VMEM((PASSES, 2, 8, 128), F32),
-                        pltpu.VMEM((PASSES, 2, 48, 256), F32), pltpu.VMEM((PASSES, 2, 8, 128), F32),
-                        pltpu.SemaphoreType.DMA((PASSES, 4)), pltpu.SemaphoreType.DMA((PASSES, 4))],
+                        pltpu.VMEM((PASSES, 3, 2, 16, 256), F32), pltpu.VMEM((PASSES, 3, 2, 8, 128), F32),
+                        pltpu.VMEM((PASSES, 3, 2, 16, 256), F32), pltpu.VMEM((PASSES, 3, 2, 8, 128), F32),
+                        pltpu.SemaphoreType.DMA((PASSES, 3, 4)), pltpu.SemaphoreType.DMA((PASSES, 3, 4))],
         compiler_params=pltpu.CompilerParams(collective_id=0, has_side_effects=True, vmem_limit_bytes=56 * 2**20),
     )(field, viscosity, speed)
 

time: 67.8 us -> 63.4 us (0.935)
  Pallas kernels: 64.3 us -> 59.9 us
    pallas_call x1, Pallas kernels: 34.8 us -> 30.7 us  [drag_(): pl.pallas_call(functools.partial(drag_kernel, unroll), out_shape=(jax.Sha...]
where the time goes in v3:
time: 63.4 us; the launch traced here: 63.2 us
  Pallas kernels  59.9 us (94%)
  local copies, waits for them, and re-layouts  2.65 us (4%)
  between operations  0.64 us (1%)
    pallas_call x1, Pallas kernels, drag_(): pl.pallas_call(functools.partial(drag_kernel, unroll), out_shape=(jax.Sha...  30.7 us
    pallas_call x1, Pallas kernels, advance(): pl.pallas_call(fluid_kernel, out_shape=jax.ShapeDtypeStruct((192, 8, 256)...  29.2 us
    unnamed x1, local copies, waits for them, and re-layouts  2.65 us

profile of v3, /device:TPU:0, one launch (start us, length us, event | category | flops | bytes accessed | tf_op | source)
XLA Modules:
  0.0 63.2 jit_solution(10888040972681915246)
XLA Ops:
  0.6 30.7 %shard_map.104 = (f32[3072,128]{1,0:T(8,128)}, f32[6,192,128]{2,1,0:T(8,128)}) custom-call(s32[1,192]{1,0:T(1,128)} %bitcast.21, s32[1,192]{1,0:T(1,128)} %bitcast.22, f32[3072,128]{1,0:T(8,128)} %bitcast.18, f32[8,256]{1,0:T(8,128)} %mass.1, f32[3,192,128]{2,1,0:T(8,128)} %bitcast.19, f32[3,192,128]{2,1,0:T(8,128)} %bitcast.20, f32[192,128]{1,0:T(8,128)} %relax.1), custom_call_target="tpu_custom_call" | custom-call | tf_op jit(solution)/shard_map/pallas_call | solution.py:155
  31.4 29.2 %shard_map.105 = f32[192,8,256]{2,1,0:T(8,128)} custom-call(f32[192,8,256]{2,1,0:T(8,128)} %bitcast.17, f32[8,256]{1,0:T(8,128)} %viscosity.1, f32[8,256]{1,0:T(8,128)} %speed.1), custom_call_target="tpu_custom_call" | custom-call | tf_op jit(solution)/shard_map/pallas_call | solution.py:306
  60.5 2.7 %copy.12 = f32[3,64,8,256]{3,2,1,0:T(8,128)} copy(f32[3,64,8,256]{3,2,1,0:T(8,128)} %bitcast.16) | data formatting | bytes 3145728

commit v4 on v3

--- a/solution.py
+++ b/solution.py
@@ -154,7 +154,7 @@
     vm = pl.BlockSpec(memory_space=pltpu.VMEM)
     return pl.pallas_call(
         functools.partial(drag_kernel, unroll),
-        out_shape=(jax.ShapeDtypeStruct((3072, 128), F32), jax.ShapeDtypeStruct((6, BINS, 128), F32)),
+        out_shape=(pltpu.VMEM((3072, 128), F32), jax.ShapeDtypeStruct((6, BINS, 128), F32)),
         in_specs=[vm] * 7,
         out_specs=(vm, vm),
         scratch_shapes=[pltpu.VMEM((GROUPS, 96, 384), BF16), pltpu.VMEM((8, BINS, 128), F32),
@@ -231,11 +231,13 @@
     return [comp * 64 + a * 16 + b * 4 + c for a in range(4) for c in range(4)]
 
 
-def fluid_kernel(field, viscosity, speed, out, ping, pong, mix, s_sec, s_air, r_sec, r_air, send_sem, recv_sem):
+def fluid_kernel(field, viscosity, speed, out, ping, pong, mix, s_sec, s_air, r_sec, r_air, s_cor, r_cor, send_sem,
+                 recv_sem):
     me_a, me_s = lax.axis_index("airway"), lax.axis_index("section")
     n_a, n_s = lax.axis_size("airway"), lax.axis_size("section")
     peers = [(me_a, lax.rem(me_s + 1, n_s)), (me_a, lax.rem(me_s + n_s - 1, n_s)),
              (lax.rem(me_a + 1, n_a), me_s), (lax.rem(me_a + n_a - 1, n_a), me_s)]
+    peers += [(peers[2 + a][0], peers[b][1]) for b in range(2) for a in range(2)]
     barrier = pltpu.get_barrier_semaphore()
     for p in peers:
         pl.semaphore_signal(barrier, inc=1, device_id=p, device_id_type=MESH)
@@ -247,10 +249,11 @@
     sub = lax.broadcasted_iota(jnp.int32, (8, 256), 0)
     lane = lax.broadcasted_iota(jnp.int32, (8, 256), 1)
     lane1 = lax.broadcasted_iota(jnp.int32, (8, 128), 1)
+    sub1 = lax.broadcasted_iota(jnp.int32, (8, 128), 0)
     some = lambda cond: jnp.where(cond, 0.25, 0.0).astype(F32)
     next_s, prev_s = some(me_s < n_s - 1), some(me_s > 0)
     next_a, prev_a = some(me_a < n_a - 1), some(me_a > 0)
-    pl.semaphore_wait(barrier, 4)
+    pl.semaphore_wait(barrier, 8)
     bufs = [field, ping, pong, ping, out]
     flying = {}
 
@@ -259,7 +262,7 @@
         for slot, row, b in ((0, 7, 3), (1, 0, 0)):
             for j, n in enumerate(sec_nodes(b, comp)):
                 s_sec[p, comp, slot, j:j + 1, :] = src[n, row:row + 1, :]
-        copies = [start(p, comp, k, s_sec, r_sec) for k in (0, 1)]
+        copies = [start(p, comp, k, s_sec.at[p, comp, k], r_sec.at[p, comp, k]) for k in range(2)]
         for slot, base, a in ((0, 128, 3), (1, 0, 0)):
             packed = jnp.zeros((8, 128), F32)
             col = 127 if slot == 0 else 0
@@ -267,19 +270,51 @@
                 moved = pltpu.roll(src[n, :, base:base + 128], (j - col) % 128, 1)
                 packed = jnp.where(lane1 == j, moved, packed)
             s_air[p, comp, slot] = packed
-        flying[p, comp] = copies + [start(p, comp, k, s_air, r_air) for k in (2, 3)]
+        copies += [start(p, comp, 2 + k, s_air.at[p, comp, k], r_air.at[p, comp, k]) for k in range(2)]
+        if p % 2 == 0:
+            for b in range(2):
+                for a in range(2):
+                    rows = s_sec[p, comp, b, 12 - 12 * a:16 - 12 * a, (1 - a) * 128:(2 - a) * 128]
+                    rows = pltpu.roll(cat([rows, rows], axis=0), 1 if a == 0 else 127, 1)
+                    s_cor[p // 2, comp, 2 * b + a, 0] = jnp.where(lane1 == 127 * a, rows, 0.0)
+                    tile = pltpu.roll(s_air[p, comp, a], 1 if b == 0 else 7, 0)
+                    tile = pltpu.roll(tile, 116 if b == 0 else 12, 1)
+                    hit = (sub1 == 7 * b) & (lane1 // 4 == 3 * b)
+                    s_cor[p // 2, comp, 2 * b + a, 1] = jnp.where(hit, tile, 0.0)
+                    k = 2 * b + a
+                    copies.append(start(p, comp, 4 + k, s_cor.at[p // 2, comp, k], r_cor.at[p // 2, comp, k]))
+        flying[p, comp] = copies
 
     def start(p, comp, k, s, r):
         copy = pltpu.make_async_remote_copy(
-            src_ref=s.at[p, comp, k % 2], dst_ref=r.at[p, comp, k % 2], send_sem=send_sem.at[p, comp, k],
-            recv_sem=recv_sem.at[p, comp, k], device_id=peers[k], device_id_type=MESH)
+            src_ref=s, dst_ref=r, send_sem=send_sem.at[p, comp, k], recv_sem=recv_sem.at[p, comp, k],
+            device_id=peers[k], device_id_type=MESH)
         copy.start()
         return copy
 
+    def complete(p, comp):
+        for c in flying[p + 1, comp]:
+            c.wait()
+        for c in flying[p, comp][4:]:
+            c.wait()
+        near = [[r_cor[p // 2, comp, 2 * b + a] for a in range(2)] for b in range(2)]
+        for slot in range(2):
+            r_sec[p + 1, comp, slot] += 0.25 * s_sec[p, comp, 1 - slot]
+            r_air[p + 1, comp, slot] += 0.25 * s_air[p, comp, 1 - slot]
+            for other in range(2):
+                scale = (prev_a, next_a)[other]
+                low = 12 * other
+                r_sec[p + 1, comp, slot, low:low + 4, other * 128:other * 128 + 128] += scale * near[slot][other][0, 0:4]
+                scale = (prev_s, next_s)[other]
+                r_air[p + 1, comp, slot] += scale * near[other][slot][1]
+
     def receive(p, comp):
         dst = bufs[p + 1]
-        for c in flying[p, comp]:
-            c.wait()
+        if p % 2 == 0:
+            for c in flying[p, comp][:4]:
+                c.wait()
+        else:
+            complete(p - 1, comp)
         for slot, row, b, scale in ((0, 0, 0, prev_s), (1, 7, 3, next_s)):
             for j, n in enumerate(sec_nodes(b, comp)):
                 dst[n, row:row + 1, :] += scale * r_sec[p, comp, slot, j:j + 1, :]
@@ -290,13 +325,20 @@
                 moved = pltpu.roll(packed, (col - j) % 128, 1)
                 dst[n, :, base:base + 128] += jnp.where(lane1 == col, moved, 0.0)
 
-    for p in range(PASSES):
+    def advance_one(p, comp):
+        section_phase(bufs[p], bufs[p + 1], visc, sub, comp)
+        airway_phase(bufs[p], bufs[p + 1], mix, lane, comp)
+
+    for p in range(0, PASSES, 2):
         for comp in range(3):
             if p:
                 receive(p - 1, comp)
             send(p, comp)
-            section_phase(bufs[p], bufs[p + 1], visc, sub, comp)
-            airway_phase(bufs[p], bufs[p + 1], mix, lane, comp)
+            advance_one(p, comp)
+            send(p + 1, comp)
+        for comp in range(3):
+            receive(p, comp)
+            advance_one(p + 1, comp)
     for comp in range(3):
         receive(PASSES - 1, comp)
 
@@ -305,15 +347,16 @@
     vm = pl.BlockSpec(memory_space=pltpu.VMEM)
     return pl.pallas_call(
         fluid_kernel,
-        out_shape=jax.ShapeDtypeStruct((192, 8, 256), F32),
+        out_shape=pltpu.VMEM((192, 8, 256), F32),
         in_specs=[vm] * 3,
         out_specs=vm,
         scratch_shapes=[pltpu.VMEM((192, 8, 256), F32), pltpu.VMEM((192, 8, 256), F32), pltpu.VMEM((12, 8, 256), F32),
                         pltpu.VMEM((PASSES, 3, 2, 16, 256), F32), pltpu.VMEM((PASSES, 3, 2, 8, 128), F32),
                         pltpu.VMEM((PASSES, 3, 2, 16, 256), F32), pltpu.VMEM((PASSES, 3, 2, 8, 128), F32),
-                        pltpu.SemaphoreType.DMA((PASSES, 3, 4)), pltpu.SemaphoreType.DMA((PASSES, 3, 4))],
+                        pltpu.VMEM((PASSES // 2, 3, 4, 2, 8, 128), F32), pltpu.VMEM((PASSES // 2, 3, 4, 2, 8, 128), F32),
+                        pltpu.SemaphoreType.DMA((PASSES, 3, 8)), pltpu.SemaphoreType.DMA((PASSES, 3, 8))],
         compiler_params=pltpu.CompilerParams(collective_id=0, has_side_effects=True, vmem_limit_bytes=56 * 2**20),
-    )(field, viscosity, speed)
+    )(pltpu.with_memory_space_constraint(field, pltpu.VMEM), viscosity, speed)
 
 def local(fluid_velocity, viscosity, axial_speed, fluid_mass, positions, velocities, relax_rates, bin_element, bin_fill):
     field = fluid_velocity.reshape(192, 8, 256)

time: 63.4 us -> 57.1 us (0.901)
  Pallas kernels: 59.9 us -> 55 us
  local copies, waits for them, and re-layouts: 2.65 us -> 1.15 us
    pallas_call x2, Pallas kernels: 59.9 us -> 55 us  [the longest x1 29.6 us: drag_(): pl.pallas_call(functools.partial(drag_kernel, unroll), out_shape=(pltpu.V...]
    unnamed x1, local copies, waits for them, and re-layouts: 2.65 us -> 1.15 us
where the time goes in v4:
time: 57.1 us; the launch traced here: 56.8 us
  Pallas kernels  55 us (96%)
  local copies, waits for them, and re-layouts  1.15 us (2%)
  between operations  0.65 us (1%)
    pallas_call x1, Pallas kernels, drag_(): pl.pallas_call(functools.partial(drag_kernel, unroll), out_shape=(pltpu.V...  29.6 us
    pallas_call x1, Pallas kernels, advance(): pl.pallas_call(fluid_kernel, out_shape=pltpu.VMEM((192, 8, 256), F32), in...  25.4 us
    unnamed x1, local copies, waits for them, and re-layouts  1.15 us

profile of v4, /device:TPU:0, one launch (start us, length us, event | category | flops | bytes accessed | tf_op | source)
XLA Modules:
  0.0 56.8 jit_solution(17869371598036658435)
XLA Ops:
  0.6 29.6 %shard_map.104 = (f32[3072,128]{1,0:T(8,128)S(1)}, f32[6,192,128]{2,1,0:T(8,128)}) custom-call(s32[1,192]{1,0:T(1,128)} %bitcast.21, s32[1,192]{1,0:T(1,128)} %bitcast.22, f32[3072,128]{1,0:T(8,128)} %bitcast.18, f32[8,256]{1,0:T(8,128)} %mass.1, f32[3,192,128]{2,1,0:T(8,128)} %bitcast.19, f32[3,192,128]{2,1,0:T(8,128)} %bitcast.20, f32[192,128]{1,0:T(8,128)} %relax.1), custom_call_target="tpu_custom_call" | custom-call | tf_op jit(solution)/shard_map/pallas_call | solution.py:155
  30.2 25.4 %shard_map.105 = f32[192,8,256]{2,1,0:T(8,128)S(1)} custom-call(f32[192,8,256]{2,1,0:T(8,128)S(1)} %bitcast.17, f32[8,256]{1,0:T(8,128)} %viscosity.1, f32[8,256]{1,0:T(8,128)} %speed.1), custom_call_target="tpu_custom_call" | custom-call | tf_op jit(solution)/shard_map/pallas_call | solution.py:348
  55.7 1.1 %copy.12 = f32[3,64,8,256]{3,2,1,0:T(8,128)} copy(f32[3,64,8,256]{3,2,1,0:T(8,128)S(1)} %bitcast.16) | data formatting | bytes 3145728

commit v5 on v4

--- a/solution.py
+++ b/solution.py
@@ -7,6 +7,8 @@
 
 F32, BF16 = jnp.float32, jnp.bfloat16
 BINS, GROUPS, SUBSTEPS = 192, 24, 16
+PASSES = 4
+MESH = pl.DeviceIdType.MESH
 cat = jnp.concatenate
 
 
@@ -43,8 +45,8 @@
     return jnp.where(same(r, c), 1.0, 0.0)
 
 
-def drag_kernel(unroll, elem, fill, fluid, mass, pos, vel, relax, coupled, pout,
-                nodal, state, acc, s_basis, s_nodal, s_first):
+def drag_part(unroll, elem, fill, fluid, mass, pos, vel, relax, coupled, pout, nodal, state, acc, s_basis, s_nodal,
+              s_first):
     diag = ones_where((BINS, 128), lambda r, c: r % 8 == c % 8)
     column = jnp.broadcast_to(elem[...].astype(F32), (128, BINS)).T
     column = cat([column, column], axis=1)
@@ -145,27 +147,14 @@
                 coupled[s, :] = fluid[s, :] - change[:, 128 * h:128 * h + 128]
 
 
-def drag(*a, **k):
-    q, p = drag_(*a, **k)
-    return q.reshape(192, 2, 8, 128).transpose(0, 2, 1, 3).reshape(192, 8, 256), p
-
-
-def drag_(fluid, mass, pos, vel, relax, elem, fill, unroll=4):
-    vm = pl.BlockSpec(memory_space=pltpu.VMEM)
-    return pl.pallas_call(
-        functools.partial(drag_kernel, unroll),
-        out_shape=(pltpu.VMEM((3072, 128), F32), jax.ShapeDtypeStruct((6, BINS, 128), F32)),
-        in_specs=[vm] * 7,
-        out_specs=(vm, vm),
-        scratch_shapes=[pltpu.VMEM((GROUPS, 96, 384), BF16), pltpu.VMEM((8, BINS, 128), F32),
-                        pltpu.VMEM((GROUPS, 128, 128), F32), pltpu.VMEM((2 * unroll, 256, 128), BF16),
-                        pltpu.VMEM((2 * unroll, 96, 128), F32), pltpu.VMEM((2 * unroll, 4, 8, 128), F32)],
-        compiler_params=pltpu.CompilerParams(vmem_limit_bytes=56 * 2**20),
-    )(elem.reshape(1, BINS), fill.reshape(1, BINS), fluid.reshape(192, 8, 2, 128).transpose(0, 2, 1, 3).reshape(3072, 128), mass, pos, vel, relax)
-
-
-PASSES = 4
-MESH = pl.DeviceIdType.MESH
+def cell(src, n, rows=slice(None)):
+    if src.shape[0] == BINS:
+        return src[n, rows]
+    return cat([src[2 * n, rows], src[2 * n + 1, rows]], axis=1)
+
+
+def half(src, n, base):
+    return src[n, :, base:base + 128] if src.shape[0] == BINS else src[2 * n + base // 128]
 
 
 def curvature(line):
@@ -185,7 +174,7 @@
 
     def body(i, _):
         base = comp * 64 + i * 16
-        t = [[src[base + 4 * b + c] for c in range(4)] for b in range(4)]
+        t = [[cell(src, base + 4 * b + c) for c in range(4)] for b in range(4)]
         across = [curvature([t[b][c] for b in range(4)]) for c in range(4)]
         for b in range(4):
             along = curvature(t[b])
@@ -209,7 +198,7 @@
         base = comp * 64 + i * 4
         for c in range(4):
             at = [base + 16 * a + c for a in range(4)]
-            q = [src[n] for n in at]
+            q = [cell(src, n) for n in at]
             d = [q[k + 1] - q[k] for k in range(3)]
             for a in range(4):
                 new = dst[at[a]] + mix[3 * a] * d[0] + mix[3 * a + 1] * d[1] + mix[3 * a + 2] * d[2]
@@ -231,8 +220,8 @@
     return [comp * 64 + a * 16 + b * 4 + c for a in range(4) for c in range(4)]
 
 
-def fluid_kernel(field, viscosity, speed, out, ping, pong, mix, s_sec, s_air, r_sec, r_air, s_cor, r_cor, send_sem,
-                 recv_sem):
+def kernel(unroll, elem, fill, fluid, mass, pos, vel, relax, viscosity, speed, out, pout, nodal, state, acc, s_basis,
+           s_nodal, s_first, field, ping, pong, mix, s_sec, s_air, r_sec, r_air, s_cor, r_cor, send_sem, recv_sem):
     me_a, me_s = lax.axis_index("airway"), lax.axis_index("section")
     n_a, n_s = lax.axis_size("airway"), lax.axis_size("section")
     peers = [(me_a, lax.rem(me_s + 1, n_s)), (me_a, lax.rem(me_s + n_s - 1, n_s)),
@@ -241,6 +230,8 @@
     barrier = pltpu.get_barrier_semaphore()
     for p in peers:
         pl.semaphore_signal(barrier, inc=1, device_id=p, device_id_type=MESH)
+    drag_part(unroll, elem, fill, fluid, mass, pos, vel, relax, field.reshape(3072, 128), pout, nodal, state, acc, s_basis,
+              s_nodal, s_first)
     visc = viscosity[...] * 2.25
     quarter = speed[...] * 0.25
     for a in range(4):
@@ -261,13 +252,13 @@
         src = bufs[p]
         for slot, row, b in ((0, 7, 3), (1, 0, 0)):
             for j, n in enumerate(sec_nodes(b, comp)):
-                s_sec[p, comp, slot, j:j + 1, :] = src[n, row:row + 1, :]
+                s_sec[p, comp, slot, j:j + 1, :] = cell(src, n, slice(row, row + 1))
         copies = [start(p, comp, k, s_sec.at[p, comp, k], r_sec.at[p, comp, k]) for k in range(2)]
         for slot, base, a in ((0, 128, 3), (1, 0, 0)):
             packed = jnp.zeros((8, 128), F32)
             col = 127 if slot == 0 else 0
             for j, n in enumerate(air_nodes(a, comp)):
-                moved = pltpu.roll(src[n, :, base:base + 128], (j - col) % 128, 1)
+                moved = pltpu.roll(half(src, n, base), (j - col) % 128, 1)
                 packed = jnp.where(lane1 == j, moved, packed)
             s_air[p, comp, slot] = packed
         copies += [start(p, comp, 2 + k, s_air.at[p, comp, k], r_air.at[p, comp, k]) for k in range(2)]
@@ -343,26 +334,29 @@
         receive(PASSES - 1, comp)
 
 
-def advance(field, viscosity, speed):
+def local(fluid_velocity, viscosity, axial_speed, fluid_mass, positions, velocities, relax_rates, bin_element, bin_fill):
+    unroll = 12
+    fluid = fluid_velocity.reshape(192, 8, 2, 128).transpose(0, 2, 1, 3).reshape(3072, 128)
     vm = pl.BlockSpec(memory_space=pltpu.VMEM)
-    return pl.pallas_call(
-        fluid_kernel,
-        out_shape=pltpu.VMEM((192, 8, 256), F32),
-        in_specs=[vm] * 3,
-        out_specs=vm,
-        scratch_shapes=[pltpu.VMEM((192, 8, 256), F32), pltpu.VMEM((192, 8, 256), F32), pltpu.VMEM((12, 8, 256), F32),
-                        pltpu.VMEM((PASSES, 3, 2, 16, 256), F32), pltpu.VMEM((PASSES, 3, 2, 8, 128), F32),
-                        pltpu.VMEM((PASSES, 3, 2, 16, 256), F32), pltpu.VMEM((PASSES, 3, 2, 8, 128), F32),
-                        pltpu.VMEM((PASSES // 2, 3, 4, 2, 8, 128), F32), pltpu.VMEM((PASSES // 2, 3, 4, 2, 8, 128), F32),
+    faces = pltpu.VMEM((PASSES, 3, 2, 16, 256), F32)
+    edges = pltpu.VMEM((PASSES, 3, 2, 8, 128), F32)
+    corners = pltpu.VMEM((PASSES // 2, 3, 4, 2, 8, 128), F32)
+    field = pltpu.VMEM((192, 8, 256), F32)
+    done, moved = pl.pallas_call(
+        functools.partial(kernel, unroll),
+        out_shape=(pltpu.VMEM((192, 8, 256), F32), pltpu.VMEM((6, BINS, 128), F32)),
+        in_specs=[vm] * 9,
+        out_specs=(vm, vm),
+        scratch_shapes=[pltpu.VMEM((GROUPS, 96, 384), BF16), pltpu.VMEM((8, BINS, 128), F32),
+                        pltpu.VMEM((GROUPS, 128, 128), F32), pltpu.VMEM((2 * unroll, 256, 128), BF16),
+                        pltpu.VMEM((2 * unroll, 96, 128), F32), pltpu.VMEM((2 * unroll, 4, 8, 128), F32),
+                        pltpu.VMEM((384, 8, 128), F32), field, field, pltpu.VMEM((12, 8, 256), F32),
+                        faces, edges, faces, edges, corners, corners,
                         pltpu.SemaphoreType.DMA((PASSES, 3, 8)), pltpu.SemaphoreType.DMA((PASSES, 3, 8))],
-        compiler_params=pltpu.CompilerParams(collective_id=0, has_side_effects=True, vmem_limit_bytes=56 * 2**20),
-    )(pltpu.with_memory_space_constraint(field, pltpu.VMEM), viscosity, speed)
-
-def local(fluid_velocity, viscosity, axial_speed, fluid_mass, positions, velocities, relax_rates, bin_element, bin_fill):
-    field = fluid_velocity.reshape(192, 8, 256)
-    coupled, moved = drag(field, fluid_mass, positions.transpose(1, 0, 2), velocities.transpose(1, 0, 2), relax_rates,
-                          bin_element, bin_fill, 12)
-    return advance(coupled, viscosity, axial_speed).reshape(fluid_velocity.shape), moved.transpose(1, 0, 2)
+        compiler_params=pltpu.CompilerParams(collective_id=0, has_side_effects=True, vmem_limit_bytes=52 * 2**20),
+    )(bin_element.reshape(1, BINS), bin_fill.reshape(1, BINS), fluid, fluid_mass, positions.transpose(1, 0, 2),
+      velocities.transpose(1, 0, 2), relax_rates, viscosity, axial_speed)
+    return done.reshape(fluid_velocity.shape), moved.transpose(1, 0, 2)
 
 
 def solution(mesh):

time: 57.1 us -> 52.5 us (0.919); the launches traced: 56.8 us -> 51.6 us
  Pallas kernels: 55 us -> 49 us
  local copies, waits for them, and re-layouts: 1.15 us -> 1.96 us
    pallas_call x2 -> x1, Pallas kernels: 55 us -> 49 us  [local(): pl.pallas_call(functools.partial(kernel, unroll), out_shape=(pltpu.VMEM((...]
    unnamed x1 -> x2, local copies, waits for them, and re-layouts: 1.15 us -> 1.96 us
where the time goes in v5:
time: 52.5 us; the launch traced here: 51.6 us
  Pallas kernels  49 us (93%)
  local copies, waits for them, and re-layouts  1.96 us (4%)
  between operations  0.64 us (1%)
    pallas_call x1, Pallas kernels, local(): pl.pallas_call(functools.partial(kernel, unroll), out_shape=(pltpu.VMEM((...  49 us
    unnamed x2, local copies, waits for them, and re-layouts  1.96 us

profile of v5, /device:TPU:0, one launch (start us, length us, event | category | flops | bytes accessed | tf_op | source)
XLA Modules:
  0.0 51.6 jit_solution(9026201595342239655)
XLA Ops:
  0.6 49.0 %shard_map.104 = (f32[192,8,256]{2,1,0:T(8,128)S(1)}, f32[6,192,128]{2,1,0:T(8,128)S(1)}) custom-call(s32[1,192]{1,0:T(1,128)} %bitcast.16, s32[1,192]{1,0:T(1,128)} %bitcast.17, f32[3072,128]{1,0:T(8,128)} %bitcast.13, f32[8,256]{1,0:T(8,128)} %mass.1, f32[3,192,128]{2,1,0:T(8,128)} %bitcast.14, f32[3,192,128]{2,1,0:T(8,128)} %bitcast.15, ...), custom_call_target="tpu_custom_call" | custom-call | tf_op jit(solution)/shard_map/pallas_call | solution.py:345
  49.6 1.1 %copy.13 = f32[3,64,8,256]{3,2,1,0:T(8,128)} copy(f32[3,64,8,256]{3,2,1,0:T(8,128)S(1)} %bitcast.11) | data formatting | bytes 3145728
  50.8 0.8 %copy.14 = f32[192,6,128]{2,0,1:T(8,128)} copy(f32[192,6,128]{2,0,1:T(8,128)S(1)} %bitcast.12) | data formatting | bytes 1179648

commit v6 on v5

--- a/solution.py
+++ b/solution.py
@@ -82,8 +82,7 @@
         lh, ll = split_tiles([b * c for b in l1 for c in l2])
         for a in range(4):
             s_first[slot, a] = l0[a]
-        s_basis[slot, 0:128] = lh
-        s_basis[slot, 128:256] = ll
+        s_basis[slot] = lh
         s_nodal[slot] = dot(nodal[g], cat([lh, ll, lh], axis=0))
 
     def second(g, slot):
@@ -101,10 +100,10 @@
             state[3 + c, rows, :] = nv
             state[c, rows, :] = jnp.clip(x[c] + stride * nv, -1.0, 1.0)
             forces += [dv * l0[a] for a in range(4)]
-        fh, fl = split_tiles(forces)
+        fh = cat([p.astype(BF16) for p in pairs(forces)], axis=0)
         wa = cat([p.astype(BF16) for p in pairs([oc * (l * l) for l in l0])], axis=0)
-        lt, llt = s_basis[slot, 0:128].T, s_basis[slot, 128:256].T
-        acc[g, 0:96] += dot(cat([fh, fl, fh], axis=1), cat([lt, lt, llt], axis=0))
+        lt = s_basis[slot].T
+        acc[g, 0:96] += dot(fh, lt)
         acc[g, 96:128] += dot(wa, lt * lt)
 
     blocks = GROUPS // unroll
@@ -348,7 +347,7 @@
         in_specs=[vm] * 9,
         out_specs=(vm, vm),
         scratch_shapes=[pltpu.VMEM((GROUPS, 96, 384), BF16), pltpu.VMEM((8, BINS, 128), F32),
-                        pltpu.VMEM((GROUPS, 128, 128), F32), pltpu.VMEM((2 * unroll, 256, 128), BF16),
+                        pltpu.VMEM((GROUPS, 128, 128), F32), pltpu.VMEM((2 * unroll, 128, 128), BF16),
                         pltpu.VMEM((2 * unroll, 96, 128), F32), pltpu.VMEM((2 * unroll, 4, 8, 128), F32),
                         pltpu.VMEM((384, 8, 128), F32), field, field, pltpu.VMEM((12, 8, 256), F32),
                         faces, edges, faces, edges, corners, corners,

time: 52.5 us -> 47.8 us (0.910)
  Pallas kernels: 49 us -> 44.3 us
    pallas_call x1, Pallas kernels: 49 us -> 44.3 us  [local(): pl.pallas_call(functools.partial(kernel, unroll), out_shape=(pltpu.VMEM((...]
where the time goes in v6:
time: 47.8 us; the launch traced here: 46.9 us
  Pallas kernels  44.3 us (93%)
  local copies, waits for them, and re-layouts  1.96 us (4%)
  between operations  0.64 us (1%)
    pallas_call x1, Pallas kernels, local(): pl.pallas_call(functools.partial(kernel, unroll), out_shape=(pltpu.VMEM((...  44.3 us
    unnamed x2, local copies, waits for them, and re-layouts  1.96 us

profile of v6, /device:TPU:0, one launch (start us, length us, event | category | flops | bytes accessed | tf_op | source)
XLA Modules:
  0.0 46.9 jit_solution(8803588273846742459)
XLA Ops:
  0.6 44.3 %shard_map.104 = (f32[192,8,256]{2,1,0:T(8,128)S(1)}, f32[6,192,128]{2,1,0:T(8,128)S(1)}) custom-call(s32[1,192]{1,0:T(1,128)} %bitcast.16, s32[1,192]{1,0:T(1,128)} %bitcast.17, f32[3072,128]{1,0:T(8,128)} %bitcast.13, f32[8,256]{1,0:T(8,128)} %mass.1, f32[3,192,128]{2,1,0:T(8,128)} %bitcast.14, f32[3,192,128]{2,1,0:T(8,128)} %bitcast.15, ...), custom_call_target="tpu_custom_call" | custom-call | tf_op jit(solution)/shard_map/pallas_call | solution.py:344
  45.0 1.1 %copy.13 = f32[3,64,8,256]{3,2,1,0:T(8,128)} copy(f32[3,64,8,256]{3,2,1,0:T(8,128)S(1)} %bitcast.11) | data formatting | bytes 3145728
  46.1 0.8 %copy.14 = f32[192,6,128]{2,0,1:T(8,128)} copy(f32[192,6,128]{2,0,1:T(8,128)S(1)} %bitcast.12) | data formatting | bytes 1179648

commit v7 on v6

--- a/solution.py
+++ b/solution.py
@@ -77,7 +77,7 @@
     acc[...] = jnp.zeros_like(acc)
 
     def first(g, slot):
-        rows = pl.ds(pl.multiple_of(g * 8, 8), 8)
+        rows = slice(g * 8, g * 8 + 8)
         l0, l1, l2 = (basis(state[i, rows, :]) for i in range(3))
         lh, ll = split_tiles([b * c for b in l1 for c in l2])
         for a in range(4):
@@ -86,7 +86,7 @@
         s_nodal[slot] = dot(nodal[g], cat([lh, ll, lh], axis=0))
 
     def second(g, slot):
-        rows = pl.ds(pl.multiple_of(g * 8, 8), 8)
+        rows = slice(g * 8, g * 8 + 8)
         x = [state[i, rows, :] for i in range(3)]
         v = [state[3 + i, rows, :] for i in range(3)]
         ro, oc = state[6, rows, :], state[7, rows, :]
@@ -110,7 +110,7 @@
 
     def run(stage, i, side):
         for j in range(unroll):
-            stage(lax.rem(i, blocks) * unroll + j, side * unroll + j)
+            stage(side * unroll + j, side * unroll + j)
 
     run(first, 0, 0)
 

time: 47.8 us -> 47.3 us (0.990)
  Pallas kernels: 44.3 us -> 43.8 us
    pallas_call x1, Pallas kernels: 44.3 us -> 43.8 us  [local(): pl.pallas_call(functools.partial(kernel, unroll), out_shape=(pltpu.VMEM((...]
where the time goes in v7:
time: 47.3 us; the launch traced here: 46.4 us
  Pallas kernels  43.8 us (93%)
  local copies, waits for them, and re-layouts  1.96 us (4%)
  between operations  0.64 us (1%)
    pallas_call x1, Pallas kernels, local(): pl.pallas_call(functools.partial(kernel, unroll), out_shape=(pltpu.VMEM((...  43.8 us
    unnamed x2, local copies, waits for them, and re-layouts  1.96 us

profile of v7, /device:TPU:0, one launch (start us, length us, event | category | flops | bytes accessed | tf_op | source)
XLA Modules:
  0.0 46.4 jit_solution(18061638445188361814)
XLA Ops:
  0.6 43.8 %shard_map.104 = (f32[192,8,256]{2,1,0:T(8,128)S(1)}, f32[6,192,128]{2,1,0:T(8,128)S(1)}) custom-call(s32[1,192]{1,0:T(1,128)} %bitcast.16, s32[1,192]{1,0:T(1,128)} %bitcast.17, f32[3072,128]{1,0:T(8,128)} %bitcast.13, f32[8,256]{1,0:T(8,128)} %mass.1, f32[3,192,128]{2,1,0:T(8,128)} %bitcast.14, f32[3,192,128]{2,1,0:T(8,128)} %bitcast.15, ...), custom_call_target="tpu_custom_call" | custom-call | tf_op jit(solution)/shard_map/pallas_call | solution.py:344
  44.5 1.1 %copy.13 = f32[3,64,8,256]{3,2,1,0:T(8,128)} copy(f32[3,64,8,256]{3,2,1,0:T(8,128)S(1)} %bitcast.11) | data formatting | bytes 3145728
  45.6 0.8 %copy.14 = f32[192,6,128]{2,0,1:T(8,128)} copy(f32[192,6,128]{2,0,1:T(8,128)S(1)} %bitcast.12) | data formatting | bytes 1179648

commit v8 on v7

--- a/solution.py
+++ b/solution.py
@@ -23,11 +23,18 @@
 
 def basis(x):
     s = x * x
-    outer = s * (9 / 16) - (1 / 16)
-    inner = s * (27 / 16) - (27 / 16)
-    ends, mids = outer * x, inner * x
-    third = inner * (1 / 3)
-    return [outer - ends, mids - third, -(mids + third), outer + ends]
+    outer, inner = s - 1 / 9, s - 1.0
+    ends, mids, third = outer * x, inner * x, inner * (1 / 3)
+    return [outer - ends, mids - third, mids + third, outer + ends]
+
+
+def node_scale(shape, axis):
+    n = lax.broadcasted_iota(jnp.int32, shape, axis)
+    scale = jnp.ones(shape, F32)
+    for shift in (4, 2, 0):
+        k = (n >> shift) & 3
+        scale = scale * jnp.where(k == 1, 27 / 16, jnp.where(k == 2, -27 / 16, 9 / 16))
+    return scale
 
 
 def pairs(tiles):
@@ -55,7 +62,7 @@
     for r in range(8):
         hot = jnp.where(cells + r * 256 == elem[...], 1.0, 0.0).astype(BF16)
         got += dot(cat(split(cat([fluid[pl.ds(8 * h + r, BINS, stride=16), :] for h in range(2)], axis=1)), axis=0), hot)
-    got = cat([got[:BINS].T, got[BINS:].T], axis=0).astype(BF16)
+    got = cat(split((got[:BINS].T + got[BINS:].T) * node_scale((BINS, BINS), 1)), axis=0)
     mask = diag.astype(BF16)
     for cp in range(6):
         rep = ones_where((BINS, 256), lambda r, c: r == cp * 32 + (c >> 3)).astype(BF16)
@@ -133,7 +140,9 @@
         two = cat([acc[:, (2 * cp + j) * 8:(2 * cp + j) * 8 + 8, :].reshape(BINS, 128) * diag for j in range(2)], axis=1)
         rep = ones_where((256, 256), lambda r, c: c == cp * 32 + (r >> 3)).astype(BF16)
         sums += dot(cat(split(two), axis=0), rep)
-    sums = cat(split((sums[:BINS] + sums[BINS:]).T), axis=1)
+    scale = node_scale((256, BINS), 0)
+    scale = cat([scale[:BINS], scale[BINS:] * scale[BINS:]], axis=0)
+    sums = cat(split((sums[:BINS] + sums[BINS:]).T * scale), axis=1)
     lanes = lax.broadcasted_iota(jnp.int32, (BINS, 256), 1).astype(F32)
     for r in range(8):
         hot = jnp.where(column == lanes + float(r * 256), 1.0, 0.0).astype(BF16)

time: 47.3 us -> 47.4 us (level)
  no operation moved by 1% of the time
where the time goes in v8:
time: 47.4 us; the launch traced here: 46.5 us
  Pallas kernels  43.9 us (93%)
  local copies, waits for them, and re-layouts  1.96 us (4%)
  between operations  0.64 us (1%)
    pallas_call x1, Pallas kernels, local(): pl.pallas_call(functools.partial(kernel, unroll), out_shape=(pltpu.VMEM((...  43.9 us
    unnamed x2, local copies, waits for them, and re-layouts  1.96 us

profile of v8, /device:TPU:0, one launch (start us, length us, event | category | flops | bytes accessed | tf_op | source)
XLA Modules:
  0.0 46.5 jit_solution(15274934300022091888)
XLA Ops:
  0.6 43.9 %shard_map.104 = (f32[192,8,256]{2,1,0:T(8,128)S(1)}, f32[6,192,128]{2,1,0:T(8,128)S(1)}) custom-call(s32[1,192]{1,0:T(1,128)} %bitcast.16, s32[1,192]{1,0:T(1,128)} %bitcast.17, f32[3072,128]{1,0:T(8,128)} %bitcast.13, f32[8,256]{1,0:T(8,128)} %mass.1, f32[3,192,128]{2,1,0:T(8,128)} %bitcast.14, f32[3,192,128]{2,1,0:T(8,128)} %bitcast.15, ...), custom_call_target="tpu_custom_call" | custom-call | tf_op jit(solution)/shard_map/pallas_call | solution.py:353
  44.6 1.1 %copy.13 = f32[3,64,8,256]{3,2,1,0:T(8,128)} copy(f32[3,64,8,256]{3,2,1,0:T(8,128)S(1)} %bitcast.11) | data formatting | bytes 3145728
  45.7 0.8 %copy.14 = f32[192,6,128]{2,0,1:T(8,128)} copy(f32[192,6,128]{2,0,1:T(8,128)S(1)} %bitcast.12) | data formatting | bytes 1179648
